TPU v7x, 512 devices: a whole 4x8x8 slice. The times are simulated.
512 devices in a mesh: ep: 128 (over z, y, core), tp: 4 (over x).
Axes of the slice: x: 4, y: 8, z: 8, core: 2. Of those that a mesh axis runs over, the one named last changes fastest.
Arguments:
- tokens: bfloat16 [2048, 2048], P('ep', 'tp'), may hold values from -6 to 6
- out_grad: bfloat16 [2048, 2048], P('ep', 'tp'), may hold values from -6 to 6
- gate_weights: bfloat16 [2048, 6], P('ep'), may hold values from 0.049804688 to 0.5
- expert_ids: int32 [2048, 6], P('ep'), may hold values from 0 to 63, all different within a row; in each aligned block of 16 rows (0 to 15, 16 to 31, ...) at most 2 rows name the same one
- w_gate: bfloat16 [128, 2048, 512], P('ep', None, 'tp'), may hold values from -0.125 to 0.125
- w_up: bfloat16 [128, 2048, 512], P('ep', None, 'tp'), may hold values from -0.125 to 0.125
- w_down: bfloat16 [128, 512, 2048], P('ep', 'tp'), may hold values from -0.1875 to 0.1875
- shared_gate: bfloat16 [2048, 1408], P('ep', 'tp'), may hold values from -0.125 to 0.125
- shared_up: bfloat16 [2048, 1408], P('ep', 'tp'), may hold values from -0.125 to 0.125
- shared_down: bfloat16 [1408, 2048], P('tp', 'ep'), may hold values from -0.15625 to 0.15625
Outputs:
- grad_tokens: bfloat16 [2048, 2048], P('ep', 'tp')
- grad_gates: float32 [2048, 6], P('ep')
- gate_grad: bfloat16 [128, 2048, 512], P('ep', None, 'tp')
- up_grad: bfloat16 [128, 2048, 512], P('ep', None, 'tp')
- down_grad: bfloat16 [128, 512, 2048], P('ep', 'tp')
Inputs may be any that keep to these rules, and one draw needn't show every extreme that they name: `expert_ids`: each row names 6 different experts. In each aligned block of 16 rows (the tokens of one index of ep) no expert is named by more than 2 rows, a bound that some block reaches.
All inputs are finite; a program needn't handle non-finite values.
Results may differ from a plain program's by a relative error of at most 0.015.
Values may be sent and summed in bfloat16 or wider, within the bound.
A program may use at most 64 MiB of HBM per device.

v0:
```python
import jax
import jax.numpy as jnp
from jax import lax
from jax.sharding import PartitionSpec as P

CAP = 2


def silu_parts(pre_gate, pre_up, back_proj, scaling):
    sigma = jax.nn.sigmoid(pre_gate)
    active = pre_gate * sigma
    hidden = active * pre_up
    scaled = scaling * back_proj
    grad_pre_gate = (scaled * pre_up * sigma * (1.0 + pre_gate * (1.0 - sigma))).astype(
        jnp.bfloat16
    )
    grad_pre_up = (scaled * active).astype(jnp.bfloat16)
    return (hidden, grad_pre_gate, grad_pre_up)


def slot_layout(expert_ids, gate_weights, experts):
    expert_range = jnp.arange(experts, dtype=jnp.int32)
    hits = (expert_ids[:, :, None] == expert_range[None, None, :]).astype(jnp.int32)
    counts = jnp.sum(hits, axis=1, dtype=jnp.int32)
    before = jnp.cumsum(counts, axis=0, dtype=jnp.int32) - counts
    position = jnp.sum(hits * before[:, None, :], axis=2, dtype=jnp.int32)
    slot_keys = expert_ids * CAP + position
    slot_range = jnp.arange(experts * CAP, dtype=jnp.int32)
    selected = slot_keys[None, :, :] == slot_range[:, None, None]
    placing = jnp.any(selected, axis=2).astype(jnp.bfloat16)
    slot_gate = jnp.sum(
        jnp.where(selected, gate_weights[None].astype(jnp.float32), 0.0), axis=(1, 2)
    )
    return (selected, placing, slot_gate.astype(jnp.bfloat16))


def to_units(rows, experts, ep_size, units_here):
    depth = rows.shape[-1]
    doubled = jnp.broadcast_to(rows.reshape(experts, 1, CAP, depth), (experts, 2, CAP, depth))
    return doubled.reshape(ep_size, units_here, CAP, depth)


def routed_part(tokens, whole_x, whole_dy, gate_weights, expert_ids, w_gate, w_up, w_down):
    ep_size = lax.axis_size("ep")
    units_here = w_gate.shape[0]
    experts = units_here * ep_size // 2
    quarter = tokens.shape[1]
    selected, placing, slot_gate = slot_layout(expert_ids, gate_weights, experts)
    gate_units = to_units(slot_gate[:, None], experts, ep_size, units_here)[..., 0]
    sent_x = jnp.dot(placing, whole_x, preferred_element_type=jnp.float32).astype(jnp.bfloat16)
    sent_dy = jnp.dot(placing, whole_dy, preferred_element_type=jnp.float32).astype(jnp.bfloat16)
    recv_x, recv_dy, recv_gate = (
        lax.all_to_all(
            to_units(sent_x, experts, ep_size, units_here),
            "ep",
            split_axis=0,
            concat_axis=0,
            tiled=True,
        ),
        lax.all_to_all(
            to_units(sent_dy, experts, ep_size, units_here),
            "ep",
            split_axis=0,
            concat_axis=0,
            tiled=True,
        ),
        lax.all_to_all(gate_units, "ep", split_axis=0, concat_axis=0, tiled=True),
    )
    pre_gate = jnp.einsum("sucd,udh->such", recv_x, w_gate, preferred_element_type=jnp.float32)
    pre_up = jnp.einsum("sucd,udh->such", recv_x, w_up, preferred_element_type=jnp.float32)
    back_proj = jnp.einsum("sucd,uhd->such", recv_dy, w_down, preferred_element_type=jnp.float32)
    scaling = recv_gate.astype(jnp.float32)[..., None]
    hidden, d_gate, d_up = silu_parts(pre_gate, pre_up, back_proj, scaling)
    router_part = jnp.sum(hidden * back_proj, axis=3)
    weighted = (scaling * hidden).astype(jnp.bfloat16)
    gate_grad = jnp.einsum(
        "sucd,such->udh", recv_x, d_gate, preferred_element_type=jnp.float32
    ).astype(jnp.bfloat16)
    up_grad = jnp.einsum("sucd,such->udh", recv_x, d_up, preferred_element_type=jnp.float32).astype(
        jnp.bfloat16
    )
    down_grad = jnp.einsum(
        "such,sucd->uhd", weighted, recv_dy, preferred_element_type=jnp.float32
    ).astype(jnp.bfloat16)
    partial_value = jnp.einsum("such,udh->sucd", d_gate, w_gate, preferred_element_type=jnp.float32)
    partial_value = partial_value + jnp.einsum(
        "such,udh->sucd", d_up, w_up, preferred_element_type=jnp.float32
    )
    reduced = lax.psum_scatter(
        partial_value.astype(jnp.bfloat16), "tp", scatter_dimension=3, tiled=True
    ).astype(jnp.float32)
    back_rows, back_router = (
        lax.all_to_all(
            reduced.astype(jnp.bfloat16), "ep", split_axis=0, concat_axis=0, tiled=True
        ).astype(reduced.dtype),
        lax.all_to_all(
            router_part.astype(jnp.bfloat16), "ep", split_axis=0, concat_axis=0, tiled=True
        ).astype(router_part.dtype),
    )
    back_rows = jnp.sum(back_rows.reshape(experts, 2, CAP, quarter), axis=1).reshape(
        experts * CAP, quarter
    )
    back_router = jnp.sum(back_router.reshape(experts, 2, CAP), axis=1).reshape(experts * CAP)
    routed = lax.dot_general(
        placing.astype(jnp.float32),
        back_rows,
        (((0,), (0,)), ((), ())),
        precision=lax.Precision.HIGHEST,
    )
    router_local = jnp.sum(jnp.where(selected, back_router[:, None, None], 0.0), axis=0)
    grad_gates = lax.psum(router_local, "tp")
    return (routed, grad_gates, gate_grad, up_grad, down_grad)


def shared_part(whole_x, whole_dy, shared_gate, shared_up, shared_down):
    full_gate, full_up = (
        lax.all_gather(shared_gate, "ep", axis=0, tiled=True),
        lax.all_gather(shared_up, "ep", axis=0, tiled=True),
    )
    full_down = lax.all_gather(shared_down, "ep", axis=1, tiled=True)
    pre_gate = jnp.dot(whole_x, full_gate, preferred_element_type=jnp.float32)
    pre_up = jnp.dot(whole_x, full_up, preferred_element_type=jnp.float32)
    back_proj = lax.dot_general(
        whole_dy, full_down, (((1,), (1,)), ((), ())), preferred_element_type=jnp.float32
    )
    unused, d_gate, d_up = silu_parts(pre_gate, pre_up, back_proj, 1.0)
    piece = lax.dot_general(
        d_gate, full_gate, (((1,), (1,)), ((), ())), preferred_element_type=jnp.float32
    )
    piece = piece + lax.dot_general(
        d_up, full_up, (((1,), (1,)), ((), ())), preferred_element_type=jnp.float32
    )
    return lax.psum_scatter(
        piece.astype(jnp.bfloat16), "tp", scatter_dimension=1, tiled=True
    ).astype(jnp.float32)


def body(
    tokens,
    out_grad,
    gate_weights,
    expert_ids,
    w_gate,
    w_up,
    w_down,
    shared_gate,
    shared_up,
    shared_down,
):
    whole_x, whole_dy = (
        lax.all_gather(tokens, "tp", axis=1, tiled=True),
        lax.all_gather(out_grad, "tp", axis=1, tiled=True),
    )
    routed, grad_gates, gate_grad, up_grad, down_grad = routed_part(
        tokens, whole_x, whole_dy, gate_weights, expert_ids, w_gate, w_up, w_down
    )
    shared = shared_part(whole_x, whole_dy, shared_gate, shared_up, shared_down)
    grad_tokens = (routed + shared).astype(jnp.bfloat16)
    return (grad_tokens, grad_gates, gate_grad, up_grad, down_grad)


def solution(mesh):
    placed = (
        P("ep", "tp"),
        P("ep", "tp"),
        P("ep", None),
        P("ep", None),
        P("ep", None, "tp"),
        P("ep", None, "tp"),
        P("ep", "tp", None),
        P("ep", "tp"),
        P("ep", "tp"),
        P("tp", "ep"),
    )
    return jax.shard_map(
        body,
        mesh=mesh,
        in_specs=placed,
        out_specs=(
            P("ep", "tp"),
            P("ep", None),
            P("ep", None, "tp"),
            P("ep", None, "tp"),
            P("ep", "tp", None),
        ),
        check_vma=False,
    )
```

profile of v0, /device:TPU:1, one launch (start us, length us, event | category | flops | bytes accessed | tf_op | source)
XLA Modules:
  0.0 331.3 jit_solution(1097779431034615973)
XLA Ops:
  8.1 0.7 all-gather.8.cloned.1.call-update
  8.7 0.8 convert_reduce_fusion.1
  9.6 0.9 select_reduce_fusion.2
  10.5 0.7 multiply_add_fusion
  11.2 10.4 %all_gather.16 = bf16[16,2048]{1,0:T(8,128)(2,1)S(1)} all-gather(bf16[16,512]{1,0:T(8,128)(2,1)} %param.10), channel_id=1, replica_groups=mesh['ep'=128,'tp'=4] {'tp'}, dimensions={1}, use_global_device_ids=true | all-gather | bytes 81920 | tf_op jit(solution)/shard_map/all_gather | solution.py:151
  21.6 0.3 convolution_convert_fusion
  22.0 0.3 broadcast_in_dim.58
  22.3 1.6 broadcast_in_dim.59
  24.0 20.5 %all-to-all-start.2 = ((bf16[128,1,2,2048]{3,2,1,0:T(2,128)(2,1)}), bf16[128,1,2,2048]{3,2,1,0:T(2,128)(2,1)S(1)}, u32[]{:S(2)}, u32[]{:S(2)}) async-start(bf16[128,1,2,2048]{3,2,1,0:T(2,128)(2,1)} %bitcast.8), calls=%async_computation.2 | async-start | bytes 2097152 | tf_op jit(solution)/shard_map/all_to_all | solution.py:53
  44.5 10.1 %all_gather.15 = bf16[16,2048]{1,0:T(8,128)(2,1)S(1)} all-gather(bf16[16,512]{1,0:T(8,128)(2,1)S(1)} %copy-done.5), channel_id=1, replica_groups=mesh['ep'=128,'tp'=4] {'tp'}, dimensions={1}, use_global_device_ids=true | all-gather | bytes 81920 | tf_op jit(solution)/shard_map/all_gather | solution.py:152
  54.5 0.3 convolution_convert_fusion.1
  54.9 0.3 broadcast_in_dim.56
  55.2 20.3 %all-to-all-done.2 = bf16[128,1,2,2048]{3,2,1,0:T(2,128)(2,1)S(1)} async-done(((bf16[128,1,2,2048]{3,2,1,0:T(2,128)(2,1)}), bf16[128,1,2,2048]{3,2,1,0:T(2,128)(2,1)S(1)}, u32[]{:S(2)}, u32[]{:S(2)}) %all-to-all-start.2) | async-done | bytes 1048608 | tf_op jit(solution)/shard_map/all_to_all | solution.py:53
  75.5 1.6 broadcast_in_dim.57
  77.2 6.6 %all-to-all-start.1 = ((bf16[128,1,2,2048]{3,2,1,0:T(2,128)(2,1)}), bf16[128,1,2,2048]{3,2,1,0:T(2,128)(2,1)S(1)}, u32[]{:S(2)}, u32[]{:S(2)}) async-start(bf16[128,1,2,2048]{3,2,1,0:T(2,128)(2,1)} %bitcast.1), calls=%async_computation.1 | async-start | bytes 2097152 | tf_op jit(solution)/shard_map/all_to_all | solution.py:60
  83.9 0.7 all-gather.4.cloned.1.call-update
  84.6 0.7 convolution_bitcast_fusion.3
  85.3 0.7 convolution_bitcast_fusion.4
  86.1 29.5 %all-to-all-done.1 = bf16[128,1,2,2048]{3,2,1,0:T(2,128)(2,1)S(1)} async-done(((bf16[128,1,2,2048]{3,2,1,0:T(2,128)(2,1)}), bf16[128,1,2,2048]{3,2,1,0:T(2,128)(2,1)S(1)}, u32[]{:S(2)}, u32[]{:S(2)}) %all-to-all-start.1) | async-done | bytes 1048608 | tf_op jit(solution)/shard_map/all_to_all | solution.py:60
  115.6 2.5 multiply_reduce_fusion
  118.0 0.8 copy.94
  118.8 7.3 %all-to-all-start.4 = ((bf16[128,1,2]{2,1,0:T(2,128)(2,1)}), bf16[128,1,2]{2,1,0:T(2,128)(2,1)S(1)}, u32[]{:S(2)}, u32[]{:S(2)}) async-start(bf16[128,1,2]{2,1,0:T(2,128)(2,1)} %copy.94), calls=%async_computation.6 | async-start | bytes 131072 | tf_op jit(solution)/shard_map/all_to_all | solution.py:96
  126.2 11.3 %all-to-all-done.4 = bf16[128,1,2]{2,1,0:T(2,128)(2,1)S(1)} async-done(((bf16[128,1,2]{2,1,0:T(2,128)(2,1)}), bf16[128,1,2]{2,1,0:T(2,128)(2,1)S(1)}, u32[]{:S(2)}, u32[]{:S(2)}) %all-to-all-start.4) | async-done | bytes 544 | tf_op jit(solution)/shard_map/all_to_all | solution.py:96
  137.8 0.2 select_reduce_fusion
  137.9 0.2 convert_element_type.101
  138.3 0.1 broadcast_in_dim.55
  138.5 0.1 copy.83
  138.6 16.8 %all_to_all.25 = bf16[128,1,2]{2,1,0:T(2,128)(2,1)S(1)} all-to-all(bf16[128,1,2]{2,1,0:T(2,128)(2,1)S(1)} %copy.83), channel_id=1, replica_groups=mesh['ep'=128,'tp'=4] {'ep'}, dimensions={0} | all-to-all | bytes 1024 | tf_op jit(solution)/shard_map/all_to_all | solution.py:67
  155.6 1.1 fusion.33
  156.6 0.5 fusion.26
  157.1 1.5 fusion.1
  158.7 0.7 all-gather.6.cloned.1.call-update
  159.4 8.7 %psum.7 = f32[16,6]{0,1:T(8,128)} all-reduce(f32[16,6]{0,1:T(8,128)S(1)} %get-tuple-element.5), channel_id=1, replica_groups=mesh['ep'=128,'tp'=4] {'tp'}, use_global_device_ids=true, to_apply=%region_11.12 | all-reduce | flops 96 | bytes 768 | tf_op jit(solution)/shard_map/psum | solution.py:111
  168.1 1.4 fusion.6
  169.4 1.4 fusion.7
  170.8 1.6 fusion.5
  172.3 1.7 fusion.50
  174.1 39.6 %all-gather.4.cloned.1.call-done = bf16[352,2048]{0,1:T(8,128)(2,1)} async-done(((bf16[352,16]{0,1:T(8,128)(2,1)}), bf16[352,2048]{0,1:T(8,128)(2,1)}) %all-gather.4.cloned.1.call-update) | async-done | bytes 1441808 | tf_op jit(solution)/shard_map/all_gather | solution.py:120
  213.7 1.7 fusion.49
  215.4 1.9 copy.91
  217.3 9.5 %all-to-all-start.3 = ((bf16[128,1,2,512]{3,2,1,0:T(2,128)(2,1)}), bf16[128,1,2,512]{3,2,1,0:T(2,128)(2,1)S(1)}, u32[]{:S(2)}, u32[]{:S(2)}) async-start(bf16[128,1,2,512]{3,2,1,0:T(2,128)(2,1)} %copy.91), calls=%async_computation.4 | async-start | bytes 524288 | tf_op jit(solution)/shard_map/all_to_all | solution.py:93
  226.9 71.0 %all-gather.6.cloned.1.call-done = bf16[2048,352]{1,0:T(8,128)(2,1)} async-done(((bf16[16,352]{1,0:T(8,128)(2,1)}), bf16[2048,352]{1,0:T(8,128)(2,1)}) %all-gather.6.cloned.1.call-update) | async-done | bytes 1441808 | tf_op jit(solution)/shard_map/all_gather | solution.py:118
  297.8 2.3 fusion.13
  300.1 2.6 fusion.8
  302.7 0.3 convert_reduce_fusion
  303.1 0.2 reshape.130
  303.2 19.4 %reduce-scatter.5.cloned.1.call-done = bf16[16,512]{1,0:T(8,128)(2,1)} async-done(((bf16[16,2048]{1,0:T(8,128)(2,1)}), bf16[16,512]{1,0:T(8,128)(2,1)}) %reduce-scatter.5.cloned.1.call-update) | async-done | bytes 16400 | tf_op jit(solution)/shard_map/reduce_scatter | solution.py:133
  322.7 1.5 fusion.11
  (35 shorter events, 1.0 us)
Async XLA Ops:
  8.0 76.6 %copy-start = (bf16[1,2048,128]{2,1,0:T(8,128)(2,1)S(1)}, bf16[1,2048,128]{2,1,0:T(8,128)(2,1)}, u32[]{:S(2)}) copy-start(bf16[1,2048,128]{2,1,0:T(8,128)(2,1)} %param.14) | copy-start | bytes 1572868
  8.0 164.3 %all-gather.8.cloned.1.call-start = ((), (), s32[]{:S(2)}) async-start(), calls=%async_computation.10 | async-start | bytes 1585152 | tf_op jit(solution)/shard_map/all_gather | solution.py:117
  22.3 22.1 %copy-start.5 = (bf16[16,512]{1,0:T(8,128)(2,1)S(1)}, bf16[16,512]{1,0:T(8,128)(2,1)}, u32[]{:S(2)}) copy-start(bf16[16,512]{1,0:T(8,128)(2,1)} %param.11) | copy-start | bytes 49156
  24.0 51.6 %all-to-all-start.2 = ((bf16[128,1,2,2048]{3,2,1,0:T(2,128)(2,1)}), bf16[128,1,2,2048]{3,2,1,0:T(2,128)(2,1)S(1)}, u32[]{:S(2)}, u32[]{:S(2)}) async-start(bf16[128,1,2,2048]{3,2,1,0:T(2,128)(2,1)} %bitcast.8), calls=%async_computation.2 | async-start | bytes 2097152 | tf_op jit(solution)/shard_map/all_to_all | solution.py:53
  77.2 8.2 %copy-start.2 = (bf16[1,2048,128]{2,1,0:T(8,128)(2,1)S(1)}, bf16[1,2048,128]{2,1,0:T(8,128)(2,1)}, u32[]{:S(2)}) copy-start(bf16[1,2048,128]{2,1,0:T(8,128)(2,1)} %param.15) | copy-start | bytes 1572868
  77.2 38.4 %all-to-all-start.1 = ((bf16[128,1,2,2048]{3,2,1,0:T(2,128)(2,1)}), bf16[128,1,2,2048]{3,2,1,0:T(2,128)(2,1)S(1)}, u32[]{:S(2)}, u32[]{:S(2)}) async-start(bf16[128,1,2,2048]{3,2,1,0:T(2,128)(2,1)} %bitcast.1), calls=%async_computation.1 | async-start | bytes 2097152 | tf_op jit(solution)/shard_map/all_to_all | solution.py:60
  83.8 129.8 %all-gather.4.cloned.1.call-start = ((), (), s32[]{:S(2)}) async-start(), calls=%async_computation.8 | async-start | bytes 1585152 | tf_op jit(solution)/shard_map/all_gather | solution.py:120
  86.1 32.7 %copy-start.3 = (f32[128,1,2,128]{0,3,2,1:T(8,128)}, f32[128,1,2,128]{0,3,2,1:T(8,128)S(1)}, u32[]{:S(2)}) copy-start(f32[128,1,2,128]{0,3,2,1:T(8,128)S(1)} %convolution_bitcast_fusion.4) | copy-start | bytes 393220
  86.1 40.1 %copy-start.6 = (bf16[16,6]{0,1:T(8,128)(2,1)S(1)}, bf16[16,6]{0,1:T(8,128)(2,1)}, u32[]{:S(2)}) copy-start(bf16[16,6]{0,1:T(8,128)(2,1)} %param.12) | copy-start | bytes 580
  118.8 18.7 %all-to-all-start.4 = ((bf16[128,1,2]{2,1,0:T(2,128)(2,1)}), bf16[128,1,2]{2,1,0:T(2,128)(2,1)S(1)}, u32[]{:S(2)}, u32[]{:S(2)}) async-start(bf16[128,1,2]{2,1,0:T(2,128)(2,1)} %copy.94), calls=%async_computation.6 | async-start | bytes 131072 | tf_op jit(solution)/shard_map/all_to_all | solution.py:96
  126.1 89.3 %reduce-scatter.3.cloned.1.call-start = ((), (), s32[]{:S(2)}) async-start(), calls=%async_computation.7 | async-start | bytes 1310720 | tf_op jit(solution)/shard_map/reduce_scatter | solution.py:89
  158.6 139.2 %all-gather.6.cloned.1.call-start = ((), (), s32[]{:S(2)}) async-start(), calls=%async_computation.9 | async-start | bytes 1585152 | tf_op jit(solution)/shard_map/all_gather | solution.py:118
  168.1 2.7 copy-start.4
  174.1 123.8 %copy-start.1 = (bf16[2048,352]{1,0:T(8,128)(2,1)S(1)}, bf16[2048,352]{1,0:T(8,128)(2,1)}, u32[]{:S(2)}) copy-start(bf16[2048,352]{1,0:T(8,128)(2,1)} %all-gather.8.cloned.1.call-done) | copy-start | bytes 4325380
  217.3 85.4 %all-to-all-start.3 = ((bf16[128,1,2,512]{3,2,1,0:T(2,128)(2,1)}), bf16[128,1,2,512]{3,2,1,0:T(2,128)(2,1)S(1)}, u32[]{:S(2)}, u32[]{:S(2)}) async-start(bf16[128,1,2,512]{3,2,1,0:T(2,128)(2,1)} %copy.91), calls=%async_computation.4 | async-start | bytes 524288 | tf_op jit(solution)/shard_map/all_to_all | solution.py:93
  226.8 95.9 %reduce-scatter.5.cloned.1.call-start = ((), (), s32[]{:S(2)}) async-start(), calls=%async_computation.11 | async-start | bytes 81920 | tf_op jit(solution)/shard_map/reduce_scatter | solution.py:133
Sparse Core Ops, SparseCore 0:
  12.5 118.2 all-gather.7
  134.5 79.1 all-gather.3
  217.4 80.4 all-gather.5
Sparse Core Ops, SparseCore 1:
  158.7 18.5 reduce-scatter.2
  302.8 19.8 reduce-scatter.4
where the time goes:
time: 333 us; the launch traced here: 331 us
  waiting for transfers between devices  193 us (58%)
  blocking collectives  46 us (14%)
  starting transfers between devices  44.1 us (13%)
  matrix products  20.7 us (6%)
  between operations  15.5 us (5%)
  local copies, waits for them, and re-layouts  7.68 us (2%)
  other arithmetic  4.26 us (1%)
    all_gather x1, waiting for transfers between devices, shared_part(): lax.all_gather(shared_up, 'ep', axis=0, tiled=True)  71 us
    all_gather x1, waiting for transfers between devices, shared_part(): full_down = lax.all_gather(shared_down, 'ep', axis=1, tiled=True)  39.6 us
    all_to_all x1, waiting for transfers between devices, routed_part(): lax.all_to_all(to_units(sent_dy, experts, ep_size, units_here), 'ep', spl...  29.5 us
    all_to_all x1, starting transfers between devices, routed_part(): lax.all_to_all(to_units(sent_x, experts, ep_size, units_here), 'ep', spli...  20.5 us
    all_to_all x1, waiting for transfers between devices, routed_part(): lax.all_to_all(to_units(sent_x, experts, ep_size, units_here), 'ep', spli...  20.3 us
    reduce_scatter x1, waiting for transfers between devices, shared_part(): lax.psum_scatter(piece.astype(jnp.bfloat16), 'tp', scatter_dimension=1, t...  19.4 us
    all_to_all x1, blocking collectives, routed_part(): lax.all_to_all(gate_units, 'ep', split_axis=0, concat_axis=0, tiled=True)  16.8 us
    all_to_all x1, waiting for transfers between devices, routed_part(): lax.all_to_all(router_part.astype(jnp.bfloat16), 'ep', split_axis=0, conc...  11.3 us
  transfers between devices with their start and end apart: 9, of which 6 were waited for; matrix products, arithmetic and copies ran while one was open for 9% of the time, Pallas kernels for 0%

commit v1 on v0

v1 whole, which is shorter than its diff:
```python
import functools

import jax
import jax.numpy as jnp
from jax import lax
from jax.experimental import pallas as pl
from jax.experimental.pallas import tpu as pltpu
from jax.sharding import PartitionSpec as P

MESH = pl.DeviceIdType.MESH
BF = jnp.bfloat16
F32 = jnp.float32
NX = 4
LANES = 128
TILES = 9
FIRST = 5


def dot(a, b, ca, cb, **kw):
    return lax.dot_general(a, b, (((ca,), (cb,)), ((), ())), preferred_element_type=F32, **kw)


def iota(shape, dim):
    return lax.broadcasted_iota(jnp.int32, shape, dim)


def one_hot(cond):
    return jnp.where(cond, 1.0, 0.0).astype(BF)


def kernel(
    n,
    tok_ref, dy_ref, gw_ref, ids_ref, wg_hbm, wu_hbm, wd_hbm, sg_ref, su_ref, sd_ref,
    gt_ref, gg_ref, ggrad_hbm, ugrad_hbm, dgrad_hbm,
    pack_a, pack_b, buf_a, buf_b, mid_a, mid_b, end_b, rx, rd,
    wg, wu, wd, ggrad, ugrad, dgrad,
    sib_out, sib_in, rs_out, rs_in, ra_out, rb_out, ra_1, rb_1, ra_mid, rb_mid, ra_2, rb_2,
    sel, s_out, sx, g1, g2, pre_out, pre_in, piece_out, piece_in, fx_out, fx_in,
    ssem, rsem, lsem,
):
    toks, feats = tok_ref.shape
    hid = wg_hbm.shape[2]
    rows = 2 * n * n
    msg = 2 * n
    half = feats // 2
    shared = sg_ref.shape[1]
    la = 3 * feats // 4

    ep = lax.axis_index("ep")
    x = lax.axis_index("tp")
    c = lax.rem(ep, 2)
    y = lax.rem(ep // 2, n)
    z = ep // (2 * n)
    sib = (ep + 1 - 2 * c, x)

    def at_y(k):
        return ((z * n + lax.rem(y + k, n)) * 2 + c, x)

    def at_z(k):
        return ((lax.rem(z + k, n) * n + y) * 2 + c, x)

    def at_x(k):
        return (ep, lax.rem(x + k, NX))

    taken = [0]
    ends = []

    def take(count):
        base = taken[0]
        taken[0] += count
        assert taken[0] <= ssem.shape[0]
        return base

    def copy(src, dst, sem, to):
        return pltpu.make_async_remote_copy(
            src_ref=src, dst_ref=dst, send_sem=ssem.at[sem], recv_sem=rsem.at[sem],
            device_id=to, device_id_type=MESH,
        )

    class Group:
        def __init__(self, count, make):
            self.count, self.make, self.base = count, make, take(count - 1)
            ends.append(self.wait_send)

        def each(self, method):
            def step(k, carry):
                getattr(self.make(k, self.base + k - 1), method)()
                return carry

            lax.fori_loop(1, self.count, step, 0)

        def start(self):
            self.each("start")

        def wait_recv(self):
            self.each("wait_recv")

        def wait_send(self):
            self.each("wait_send")

    def single(src, dst, to):
        made = copy(src, dst, take(1), to)
        ends.append(made.wait_send)
        return made

    loads = [
        pltpu.make_async_copy(a.at[0], b, lsem.at[i])
        for i, (a, b) in enumerate(((wg_hbm, wg), (wu_hbm, wu), (wd_hbm, wd)))
    ]
    for load in loads:
        load.start()

    barrier = pltpu.get_barrier_semaphore()

    def greet(k, carry):
        for to in (at_y(k), at_z(k)):
            pl.semaphore_signal(barrier, inc=1, device_id=to, device_id_type=MESH)
        return carry

    lax.fori_loop(1, n, greet, 0)
    for k in range(NX):
        if k:
            pl.semaphore_signal(barrier, inc=1, device_id=at_x(k), device_id_type=MESH)
        pl.semaphore_signal(
            barrier, inc=1, device_id=(sib[0], lax.rem(x + k, NX)), device_id_type=MESH
        )

    ids = ids_ref[...]
    gates = gw_ref[...].astype(F32)
    lane = iota((toks, rows), 1)
    slot = lane % 2
    outer, inner = lane // msg, (lane // 2) % n
    earlier = one_hot(iota((toks, toks), 0) > iota((toks, toks), 1))

    def place(expert):
        named = [ids[:, k : k + 1] == expert for k in range(ids.shape[1])]
        hits = functools.reduce(jnp.logical_or, named)
        before = dot(earlier, one_hot(hits), 1, 0)
        here = jnp.logical_and(hits, before == slot.astype(F32))
        weight = sum(
            jnp.where(named[k], gates[:, k : k + 1], 0.0) for k in range(len(named))
        )
        return named, here, weight

    named_a, here_a, _ = place(((z + outer) % n) * n + (y + inner) % n)
    _, here_b, weight_b = place(((z + inner) % n) * n + (y + outer) % n)
    place_a = one_hot(here_a)
    place_b = one_hot(here_b)
    put_a = jnp.where(here_a, 1.0, 0.0).T.astype(BF)
    put_b = jnp.where(here_b, weight_b, 0.0).T.astype(BF)
    tok = tok_ref[...]
    dy = dy_ref[...]
    pack_a[...] = dot(put_a, tok, 1, 0).astype(BF).reshape(n, msg, feats)
    pack_b[...] = dot(put_b, dy, 1, 0).astype(BF).reshape(n, msg, feats)

    turned_row = iota((rows, rows), 0)
    turned = ((turned_row // 2) % n) * msg + (turned_row // msg) * 2 + turned_row % 2
    turn = one_hot(iota((rows, rows), 1) == turned)

    col = iota((feats, feats), 1)
    col_in = col % half
    feature = 32 * (col_in // 16) + 16 * (col // half) + col_in % 16
    sel[...] = one_hot(iota((feats, feats), 0) == feature)
    s_all = dot(jnp.concatenate([tok, dy], axis=0), sel[...], 1, 0).astype(BF)
    s_out[0] = s_all[:, :half]
    s_out[1] = s_all[:, half:]

    eye = one_hot(iota((16, 16), 0) == iota((16, 16), 1))
    sd_t = dot(eye, sd_ref[...], 1, 1).astype(BF)
    tiles = []
    for block in (sg_ref[...], su_ref[...], sd_t):
        pad = jnp.zeros((16, TILES // 3 * LANES - shared), BF)
        block = jnp.concatenate([block, pad], axis=1)
        tiles += [block[:, i * LANES : (i + 1) * LANES] for i in range(TILES // 3)]
    for i, tile in enumerate(tiles):
        if i < FIRST:
            g1[y, z, i] = tile
        else:
            g2[z, y, i - FIRST] = tile

    pl.semaphore_wait(barrier, 2 * (n - 1) + 2 * NX - 1)

    a1 = Group(n, lambda k, s: copy(pack_a.at[k], buf_a.at[k], s, at_z(k)))
    b1 = Group(n, lambda k, s: copy(pack_b.at[k], buf_b.at[k], s, at_y(k)))
    a1.start()
    b1.start()
    s_same = Group(NX, lambda k, s: copy(s_out.at[c], sx.at[c, x], s, at_x(k)))
    s_same.start()
    s_other = [
        single(s_out.at[1 - c], sx.at[c, x], (sib[0], lax.rem(x + k, NX))) for k in range(NX)
    ]
    for made in s_other:
        made.start()
    sx[c, x] = s_out[c]
    w1 = Group(n, lambda k, s: copy(g1.at[y, z], g1.at[y, z], s, at_z(k)))
    w2 = Group(n, lambda k, s: copy(g2.at[z, y], g2.at[z, y], s, at_y(k)))
    w1.start()
    w2.start()

    buf_a[0] = pack_a[0]
    buf_b[0] = pack_b[0]

    a1.wait_recv()
    mid_a[...] = dot(turn, buf_a[...].reshape(rows, feats), 1, 0).astype(BF).reshape(n, msg, feats)

    def part(k):
        return pl.ds(pl.multiple_of(k * msg, msg), msg)

    a2 = Group(n, lambda k, s: copy(mid_a.at[k], rx.at[c, x, part(k)], s, at_y(k)))
    a2.start()
    rx[c, x, 0:msg] = mid_a[0]
    b1.wait_recv()
    mid_b[...] = dot(turn, buf_b[...].reshape(rows, feats), 1, 0).astype(BF).reshape(n, msg, feats)
    b2 = Group(n, lambda k, s: copy(mid_b.at[k], end_b.at[k], s, at_z(k)))
    b2.start()
    end_b[0] = mid_b[0]

    class Ring:
        def __init__(self, buf, pos, go):
            self.buf, self.pos, self.go, self.step = buf, pos, go, 0
            self.flying = []

        def block(self, k):
            return lax.rem(self.pos + k + 2 * n, n)

        def forward(self):
            for made in self.flying:
                made.wait_recv()
            s = self.step
            self.flying = []
            if s < n // 2 - 1:
                for way in (1, -1):
                    at = self.buf.at[self.block(-way * s)]
                    self.flying.append(single(at, at, self.go(way % n)))
            elif s == n // 2 - 1:
                for way in (1, -1):
                    span = pl.ds(0, n // 2) if way == 1 else pl.ds(n // 2, n // 2)
                    at = self.buf.at[self.block(-way * s), span]
                    self.flying.append(single(at, at, self.go(way % n)))
            for made in self.flying:
                made.start()
            self.step += 1

    ring1 = Ring(g1, y, at_y)
    ring2 = Ring(g2, z, at_z)
    w1.wait_recv()
    ring1.forward()
    w2.wait_recv()
    ring2.forward()

    a2.wait_recv()
    mine_x = rx.at[c, x]
    x_right = single(mine_x, mine_x, at_x(1))
    x_left = single(mine_x, mine_x, at_x(NX - 1))
    x_sib = Group(NX + 1, lambda k, s: copy(
        rx.at[c, lax.rem(x + k - 1, NX)], rx.at[c, lax.rem(x + k - 1, NX)], s, sib))
    d_sib = Group(NX + 1, lambda k, s: copy(
        rd.at[c, lax.rem(x + k - 1, NX)], rd.at[c, lax.rem(x + k - 1, NX)], s, sib))

    def to_sib(group, k):
        group.make(k + 1, group.base + k).start()

    x_right.start()
    x_left.start()
    to_sib(x_sib, 0)
    b2.wait_recv()
    rd[c, x] = dot(turn, end_b[...].reshape(rows, feats), 1, 0).astype(BF)
    mine_d = rd.at[c, x]
    d_right = single(mine_d, mine_d, at_x(1))
    d_left = single(mine_d, mine_d, at_x(NX - 1))
    d_right.start()
    d_left.start()
    to_sib(d_sib, 0)

    ring1.forward()
    ring2.forward()

    from_left = lax.rem(x + NX - 1, NX)
    from_right = lax.rem(x + 1, NX)
    x_right.wait_recv()
    x_on = single(rx.at[c, from_left], rx.at[c, from_left], at_x(1))
    x_on.start()
    to_sib(x_sib, 3)
    x_left.wait_recv()
    to_sib(x_sib, 1)
    d_left.wait_recv()
    d_on = single(rd.at[c, from_right], rd.at[c, from_right], at_x(NX - 1))
    d_on.start()
    to_sib(d_sib, 1)
    d_right.wait_recv()
    to_sib(d_sib, 3)

    ring1.forward()
    ring2.forward()

    x_on.wait_recv()
    to_sib(x_sib, 2)
    d_on.wait_recv()
    to_sib(d_sib, 2)

    ring1.forward()
    ring2.forward()

    for load in loads:
        load.wait()
    x_sib.wait_recv()
    d_sib.wait_recv()

    def quarter(ref, q):
        return jnp.concatenate([ref[0, q], ref[1, q]], axis=0)

    def w_quarter(q):
        span = slice(q * feats, (q + 1) * feats)
        return jnp.concatenate([wg[span], wu[span]], axis=1)

    pre = sum(dot(quarter(rx, q), w_quarter(q), 1, 0) for q in range(NX))
    q_back = sum(
        dot(quarter(rd, q), wd[:, q * feats : (q + 1) * feats], 1, 1) for q in range(NX)
    )

    def silu_parts(pre_gate, pre_up, back):
        sigma = jax.nn.sigmoid(pre_gate)
        active = pre_gate * sigma
        d_gate = back * pre_up * sigma * (1.0 + pre_gate * (1.0 - sigma))
        return active * pre_up, jnp.concatenate([d_gate, back * active], axis=1).astype(BF)

    hidden, d_both = silu_parts(pre[:, :hid], pre[:, hid:], q_back)
    router = jnp.sum(hidden * q_back, axis=1, keepdims=True)
    hidden = hidden.astype(BF)

    def coded(value):
        first = value.astype(BF).astype(F32)
        at = iota((value.shape[0], LANES), 1)
        return jnp.where(at == 0, first, jnp.where(at == 1, value - first, 0.0)).astype(BF)

    first_half = c == 0
    d_own = jnp.where(first_half, d_both[:rows], d_both[rows:])
    d_sibs = jnp.where(first_half, d_both[rows:], d_both[:rows])
    r_own = jnp.where(first_half, router[:rows], router[rows:])
    r_sibs = jnp.where(first_half, router[rows:], router[:rows])

    for q in range(NX):
        sib_out[:, q * feats : (q + 1) * feats] = dot(d_sibs, w_quarter(q), 1, 1).astype(BF)
    sib_out[:, NX * feats :] = coded(r_sibs)
    part_sib = single(sib_out, sib_in, sib)
    part_sib.start()
    own = [dot(d_own, w_quarter(q), 1, 1) for q in range(NX)]
    part_sib.wait_recv()
    r_chip = r_own + jnp.sum(sib_in[:, NX * feats :].astype(F32), axis=1, keepdims=True)
    r_coded = coded(r_chip)
    for q in range(NX):
        total = own[q] + sib_in[:, q * feats : (q + 1) * feats].astype(F32)
        rs_out[q, :, :feats] = total.astype(BF)
        rs_out[q, :, feats:] = r_coded
    rs = Group(NX, lambda k, s: copy(
        rs_out.at[lax.rem(x + k, NX)], rs_in.at[k], s, at_x(k)))
    rs.start()

    stores = []
    for i, (a, b) in enumerate(((ggrad, ggrad_hbm), (ugrad, ugrad_hbm), (dgrad, dgrad_hbm))):
        stores.append(pltpu.make_async_copy(a, b.at[0], lsem.at[3 + i]))
    for q in range(NX):
        span = slice(q * feats, (q + 1) * feats)
        both = dot(quarter(rx, q), d_both, 0, 0).astype(BF)
        ggrad[span] = both[:, :hid]
        ugrad[span] = both[:, hid:]
        dgrad[:, span] = dot(hidden, quarter(rd, q), 0, 0).astype(BF)
    for store in stores:
        store.start()

    rs.wait_recv()
    summed = rs_out[x].astype(F32)
    for k in range(1, NX):
        summed = summed + rs_in[k].astype(F32)
    r_total = coded(jnp.sum(summed[:, feats:], axis=1, keepdims=True))
    ra_out[...] = summed[:, :la].astype(BF).reshape(n, msg, la)
    rest = jnp.concatenate([summed[:, la:feats].astype(BF), r_total], axis=1)
    lb = rest.shape[1]
    rb_out[...] = dot(turn, rest, 1, 0).astype(BF).reshape(n, msg, lb)
    back_a1 = Group(n, lambda k, s: copy(ra_out.at[k], ra_1.at[k], s, at_y(n - k)))
    back_b1 = Group(n, lambda k, s: copy(rb_out.at[k], rb_1.at[k], s, at_z(n - k)))
    back_a1.start()
    back_b1.start()
    ra_1[0] = ra_out[0]
    rb_1[0] = rb_out[0]

    ring1.forward()
    ring2.forward()
    s_same.wait_recv()
    for made in s_other:
        made.wait_recv()

    def weights(i):
        if i < FIRST:
            parts = [g1[:, k, i].reshape(n * 16, LANES) for k in range(n)]
        else:
            parts = [g2[k, :, i - FIRST].reshape(n * 16, LANES) for k in range(n)]
        return jnp.concatenate(parts, axis=0)

    def matrix(m):
        return jnp.concatenate([weights(3 * m + i) for i in range(3)], axis=1)

    def features(low):
        return jnp.concatenate(
            [
                jnp.concatenate([sx[s, q, low : low + toks] for q in range(NX)], axis=1)
                for s in range(2)
            ],
            axis=0,
        )

    width = 3 * LANES
    s_tok = features(0)
    s_dy = features(toks)
    pre_out[:, :width] = dot(s_tok, matrix(0), 1, 0)
    pre_out[:, width : 2 * width] = dot(s_tok, matrix(1), 1, 0)
    pre_out[:, 2 * width :] = dot(s_dy, matrix(2), 1, 0)
    pre_sib = single(pre_out, pre_in, sib)
    pre_sib.start()

    back_a1.wait_recv()
    ra_mid[...] = dot(turn, ra_1[...].reshape(rows, la), 1, 0).astype(BF).reshape(n, msg, la)
    back_a2 = Group(n, lambda k, s: copy(ra_mid.at[k], ra_2.at[k], s, at_z(n - k)))
    back_a2.start()
    ra_2[0] = ra_mid[0]
    back_b1.wait_recv()
    rb_mid[...] = dot(turn, rb_1[...].reshape(rows, lb), 1, 0).astype(BF).reshape(n, msg, lb)
    back_b2 = Group(n, lambda k, s: copy(rb_mid.at[k], rb_2.at[k], s, at_y(n - k)))
    back_b2.start()
    rb_2[0] = rb_mid[0]

    pre_sib.wait_recv()
    s_pre = pre_out[...] + pre_in[...]
    _, s_both = silu_parts(s_pre[:, :width], s_pre[:, width : 2 * width], s_pre[:, 2 * width :])
    piece = dot(s_both[:, :width], matrix(0), 1, 1) + dot(s_both[:, width:], matrix(1), 1, 1)
    for q in range(NX):
        piece_out[q] = piece[:, q * half : (q + 1) * half].astype(BF)
    s_rs = Group(NX, lambda k, s: copy(
        piece_out.at[lax.rem(x + k, NX)], piece_in.at[k], s, at_x(k)))
    s_rs.start()
    s_rs.wait_recv()
    s_sum = piece_out[x].astype(F32)
    for k in range(1, NX):
        s_sum = s_sum + piece_in[k].astype(F32)
    s_sum = s_sum.astype(BF)
    s_own = jnp.where(first_half, s_sum[:toks], s_sum[toks:])
    fx_out[...] = jnp.where(first_half, s_sum[toks:], s_sum[:toks])
    s_fx = single(fx_out, fx_in, sib)
    s_fx.start()

    back_a2.wait_recv()
    back_b2.wait_recv()
    ret_b = rb_2[...].reshape(rows, lb)
    routed = jnp.concatenate(
        [
            dot(place_a, ra_2[...].reshape(rows, la), 1, 0),
            dot(place_b, ret_b[:, : feats - la], 1, 0),
        ],
        axis=1,
    )
    expert_b = ((z + inner) % n) * n + (y + outer) % n
    picked = jnp.concatenate(
        [
            one_hot(jnp.logical_and(here_b, ids[:, k : k + 1] == expert_b))
            for k in range(ids.shape[1])
        ],
        axis=0,
    )
    routers = jnp.sum(dot(picked, ret_b[:, feats - la :], 1, 0), axis=1, keepdims=True)
    gg_ref[...] = jnp.concatenate(
        [routers[k * toks : (k + 1) * toks] for k in range(ids.shape[1])], axis=1
    ) / gates
    s_fx.wait_recv()
    s_other_half = fx_in[...]
    both_halves = jnp.concatenate(
        [
            jnp.where(first_half, s_own, s_other_half),
            jnp.where(first_half, s_other_half, s_own),
        ],
        axis=1,
    )
    gt_ref[...] = (routed + dot(both_halves, sel[...], 1, 1)).astype(BF)

    for store in stores:
        store.wait()
    for end in ends:
        end()


def body(tokens, out_grad, gate_weights, expert_ids, w_gate, w_up, w_down, s_gate, s_up, s_down):
    n = round((lax.axis_size("ep") // 2) ** 0.5)
    toks, feats = tokens.shape
    hid = w_gate.shape[2]
    rows, msg, half = 2 * n * n, 2 * n, feats // 2
    la = 3 * feats // 4
    lb = feats + LANES - la
    vmem = pl.BlockSpec(memory_space=pltpu.VMEM)
    hbm = pl.BlockSpec(memory_space=pl.ANY)

    def legs(lanes, count):
        return [pltpu.VMEM((n, msg, lanes), BF) for _ in range(count)]

    def like(a):
        return jax.ShapeDtypeStruct(a.shape, a.dtype)

    scratch = (
        legs(feats, 7)
        + [pltpu.VMEM((2, NX, rows, feats), BF)] * 2
        + [pltpu.VMEM(a.shape[1:], BF) for a in (w_gate, w_up, w_down)] * 2
        + [pltpu.VMEM((rows, NX * feats + LANES), BF)] * 2
        + [pltpu.VMEM((NX, rows, feats + LANES), BF)] * 2
        + legs(la, 1) + legs(lb, 1) + legs(la, 1) + legs(lb, 1)
        + legs(la, 1) + legs(lb, 1) + legs(la, 1) + legs(lb, 1)
        + [
            pltpu.VMEM((feats, feats), BF),
            pltpu.VMEM((2, 2 * toks, half), BF),
            pltpu.VMEM((2, NX, 2 * toks, half), BF),
            pltpu.VMEM((n, n, FIRST, 16, LANES), BF),
            pltpu.VMEM((n, n, TILES - FIRST, 16, LANES), BF),
            pltpu.VMEM((2 * toks, TILES * LANES), F32),
            pltpu.VMEM((2 * toks, TILES * LANES), F32),
            pltpu.VMEM((NX, 2 * toks, half), BF),
            pltpu.VMEM((NX, 2 * toks, half), BF),
            pltpu.VMEM((toks, half), BF),
            pltpu.VMEM((toks, half), BF),
            pltpu.SemaphoreType.DMA((140,)),
            pltpu.SemaphoreType.DMA((140,)),
            pltpu.SemaphoreType.DMA((6,)),
        ]
    )
    return pl.pallas_call(
        functools.partial(kernel, n),
        out_shape=(
            like(tokens),
            jax.ShapeDtypeStruct(gate_weights.shape, F32),
            like(w_gate),
            like(w_up),
            like(w_down),
        ),
        in_specs=[vmem] * 4 + [hbm] * 3 + [vmem] * 3,
        out_specs=(vmem, vmem, hbm, hbm, hbm),
        scratch_shapes=scratch,
        compiler_params=pltpu.CompilerParams(
            collective_id=0, has_side_effects=True, vmem_limit_bytes=48 * 1024 * 1024
        ),
    )(tokens, out_grad, gate_weights, expert_ids, w_gate, w_up, w_down, s_gate, s_up, s_down)


def solution(mesh):
    placed = (
        P("ep", "tp"),
        P("ep", "tp"),
        P("ep", None),
        P("ep", None),
        P("ep", None, "tp"),
        P("ep", None, "tp"),
        P("ep", "tp", None),
        P("ep", "tp"),
        P("ep", "tp"),
        P("tp", "ep"),
    )
    return jax.shard_map(
        body,
        mesh=mesh,
        in_specs=placed,
        out_specs=(
            P("ep", "tp"),
            P("ep", None),
            P("ep", None, "tp"),
            P("ep", None, "tp"),
            P("ep", "tp", None),
        ),
        check_vma=False,
    )
```

time: 333 us -> 78.6 us (0.24)
  waiting for transfers between devices: 193 us -> 0 us
  Pallas kernels: 0 us -> 68.5 us
  blocking collectives: 46 us -> 0 us
  starting transfers between devices: 44.1 us -> 0 us
  matrix products: 20.7 us -> 0 us
  between operations: 15.5 us -> 0.67 us
  other arithmetic: 4.26 us -> 0 us
    all_gather x3 -> x0, waiting for transfers between devices: 111 us -> none  [the longest x1 71 us: shared_part(): lax.all_gather(shared_up, 'ep', axis=0, tiled=True)]
    pallas_call x0 -> x1, Pallas kernels: none -> 68.5 us  [body(): pl.pallas_call(functools.partial(kernel, n), out_shape=(like(tokens), jax...]
    all_to_all x4 -> x0, waiting for transfers between devices: 61.1 us -> none  [the longest x1 29.5 us: routed_part(): lax.all_to_all(to_units(sent_dy, experts, ep_size, units_here), 'ep', spl...]
    all_to_all x4 -> x0, starting transfers between devices: 43.9 us -> none  [the longest x1 20.5 us: routed_part(): lax.all_to_all(to_units(sent_x, experts, ep_size, units_here), 'ep', spli...]
    dot_general x15 -> x0, matrix products: 20.7 us -> none  [the longest x1 2.58 us: shared_part(): lax.dot_general(d_up, full_up, (((1,), (1,)), ((), ())), preferred_elemen...]
    all_gather x2 -> x0, blocking collectives: 20.4 us -> none  [the longest x1 10.4 us: body(): lax.all_gather(tokens, 'tp', axis=1, tiled=True)]
    reduce_scatter x2 -> x0, waiting for transfers between devices: 19.5 us -> none  [the longest x1 19.4 us: shared_part(): lax.psum_scatter(piece.astype(jnp.bfloat16), 'tp', scatter_dimension=1, t...]
    all_to_all x1 -> x0, blocking collectives: 16.8 us -> none  [routed_part(): lax.all_to_all(gate_units, 'ep', split_axis=0, concat_axis=0, tiled=True)]
  transfers between devices with their start and end apart: 9 -> 0, of which waited for: 6 -> 0; matrix products, arithmetic and copies ran while one was open for 9% -> 0% of each run, Pallas kernels for 0% -> 0%
where the time goes in v1:
time: 78.6 us; the launch traced here: 78.2 us
  Pallas kernels  68.5 us (87%)
  local copies, waits for them, and re-layouts  9.06 us (12%)
    pallas_call x1, Pallas kernels, body(): pl.pallas_call(functools.partial(kernel, n), out_shape=(like(tokens), jax...  68.5 us
    unnamed x23, local copies, waits for them, and re-layouts  8.39 us

profile of v1, /device:TPU:1, one launch (start us, length us, event | category | flops | bytes accessed | tf_op | source)
XLA Modules:
  0.0 78.2 jit_solution(4891617734402532250)
XLA Ops:
  0.6 0.0 copy-start.7
  0.6 0.8 copy.15.gw_ref
  1.4 0.8 copy.16.ids_ref
  2.2 0.0 copy-done.7
  2.2 0.0 copy-start.3
  2.2 0.0 copy-start.4
  2.2 0.0 copy-start.5
  2.2 0.0 copy-start.6
  2.2 0.1 copy.17.sd_ref
  2.3 0.6 copy-done.3
  2.9 0.0 copy-done.4
  2.9 0.0 copy-done.5
  2.9 0.0 copy-done.6
  2.9 0.0 copy-start
  2.9 1.0 %copy-done = bf16[1,2048,128]{2,1,0:T(8,128)(2,1)S(1)} copy-done((bf16[1,2048,128]{2,1,0:T(8,128)(2,1)S(1)}, bf16[1,2048,128]{2,1,0:T(8,128)(2,1)}, u32[]{:S(2)}) %copy-start) | copy-done | bytes 524312
  4.0 0.0 copy-start.1
  4.0 1.0 %copy-done.1 = bf16[1,2048,128]{2,1,0:T(8,128)(2,1)S(1)} copy-done((bf16[1,2048,128]{2,1,0:T(8,128)(2,1)S(1)}, bf16[1,2048,128]{2,1,0:T(8,128)(2,1)}, u32[]{:S(2)}) %copy-start.1) | copy-done | bytes 524312
  5.0 0.0 copy-start.2
  5.0 1.0 %copy-done.2 = bf16[1,128,2048]{2,1,0:T(8,128)(2,1)S(1)} copy-done((bf16[1,128,2048]{2,1,0:T(8,128)(2,1)S(1)}, bf16[1,128,2048]{2,1,0:T(8,128)(2,1)}, u32[]{:S(2)}) %copy-start.2) | copy-done | bytes 524312
  6.1 68.5 %shard_map.137 = (bf16[16,512]{1,0:T(8,128)(2,1)S(1)}, f32[16,6]{1,0:T(8,128)S(1)}, bf16[1,2048,128]{2,1,0:T(8,128)(2,1)S(1)}, bf16[1,2048,128]{2,1,0:T(8,128)(2,1)S(1)}, bf16[1,128,2048]{2,1,0:T(8,128)(2,1)S(1)}) custom-call(bf16[16,512]{1,0:T(8,128)(2,1)S(1)} %copy-done.3, bf16[16,512]{1,0:T(8,128)(2,1)S(1)} %copy-done.4, bf16[16,6]{1,0:T(8,128)(2,1)S(1)} %copy.15.gw_ref, ...), custom_call_target="tpu_custom_call" | custom-call | tf_op jit(solution)/shard_map/pallas_call | solution.py:531
  74.6 0.7 copy.18
  75.3 0.6 copy.23
  75.9 0.8 %copy.24 = bf16[1,2048,128]{2,1,0:T(8,128)(2,1)} copy(bf16[1,2048,128]{2,1,0:T(8,128)(2,1)S(1)} %get-tuple-element.17) | data formatting | bytes 1048576
  76.7 0.8 %copy.25 = bf16[1,2048,128]{2,1,0:T(8,128)(2,1)} copy(bf16[1,2048,128]{2,1,0:T(8,128)(2,1)S(1)} %get-tuple-element.18) | data formatting | bytes 1048576
  77.5 0.8 %copy.26 = bf16[1,128,2048]{2,1,0:T(8,128)(2,1)} copy(bf16[1,128,2048]{2,1,0:T(8,128)(2,1)S(1)} %get-tuple-element.19) | data formatting | bytes 1048576
Async XLA Ops:
  0.6 1.6 %copy-start.7 = (bf16[352,16]{0,1:T(8,128)(2,1)S(1)}, bf16[352,16]{0,1:T(8,128)(2,1)}, u32[]{:S(2)}) copy-start(bf16[352,16]{0,1:T(8,128)(2,1)} %param.19) | copy-start | bytes 33796
  2.2 0.7 copy-start.3
  2.2 0.7 copy-start.4
  2.2 0.7 copy-start.5
  2.2 0.7 copy-start.6
  2.9 1.0 %copy-start = (bf16[1,2048,128]{2,1,0:T(8,128)(2,1)S(1)}, bf16[1,2048,128]{2,1,0:T(8,128)(2,1)}, u32[]{:S(2)}) copy-start(bf16[1,2048,128]{2,1,0:T(8,128)(2,1)} %wg_hbm.1) | copy-start | bytes 1572868
  4.0 1.0 %copy-start.1 = (bf16[1,2048,128]{2,1,0:T(8,128)(2,1)S(1)}, bf16[1,2048,128]{2,1,0:T(8,128)(2,1)}, u32[]{:S(2)}) copy-start(bf16[1,2048,128]{2,1,0:T(8,128)(2,1)} %wu_hbm.1) | copy-start | bytes 1572868
  5.0 1.0 %copy-start.2 = (bf16[1,128,2048]{2,1,0:T(8,128)(2,1)S(1)}, bf16[1,128,2048]{2,1,0:T(8,128)(2,1)}, u32[]{:S(2)}) copy-start(bf16[1,128,2048]{2,1,0:T(8,128)(2,1)} %wd_hbm.1) | copy-start | bytes 1572868

commit v2 on v1

v2 whole, which is shorter than its diff:
```python
import functools
import math

import jax
import jax.numpy as jnp
from jax import lax
from jax.experimental import pallas as pl
from jax.experimental.pallas import tpu as pltpu
from jax.sharding import PartitionSpec as P

MESH = pl.DeviceIdType.MESH
BF = jnp.bfloat16
F32 = jnp.float32
NX = 4
LIMIT = 60 * 1024 * 1024
LANES = 128
TILES = 9
FIRST = 5


def dot(a, b, ca, cb, **kw):
    return lax.dot_general(a, b, (((ca,), (cb,)), ((), ())), preferred_element_type=F32, **kw)


def iota(shape, dim):
    return lax.broadcasted_iota(jnp.int32, shape, dim)


def one_hot(cond):
    return jnp.where(cond, 1.0, 0.0).astype(BF)


def kernel(
    n,
    tok_hbm, dy_hbm, gw_hbm, ids_hbm, wg_hbm, wu_hbm, wd_hbm, sg_hbm, su_hbm, sd_hbm,
    gt_hbm, gg_hbm, ggrad_hbm, ugrad_hbm, dgrad_hbm,
    gt_ref, gg_ref, ggrad, ugrad, dgrad, tok_ref, dy_ref, gw_ref, ids_ref, sg_ref, su_ref, sd_ref,
    pack_a, pack_b, buf_a, buf_b, mid_a, mid_b, rx, rd, wg, wu, wd,
    sib_out, sib_in, rs_out, rs_in, rt_out, rt_in, rr_out, rr_in, ret_out, ret_1, ret_mid, ret_2,
    sel, s_out, sx, g1, g2, pre_out, pre_in, piece_out, piece_in, fx_out, fx_in, tally,
    ssem, rsem, lsem,
):
    toks, feats = tok_ref.shape
    hid = wg_hbm.shape[2]
    rows = 2 * n * n
    msg = 2 * n
    half = feats // 2
    shared = sg_ref.shape[1]
    top = ids_ref.shape[0]
    edges = sorted({0, min(3, n), min(5, n), n})
    chunks = list(zip(edges, edges[1:]))

    ep = lax.axis_index("ep")
    x = lax.axis_index("tp")
    c = lax.rem(ep, 2)
    y = lax.rem(ep // 2, n)
    z = ep // (2 * n)
    sib = (ep + 1 - 2 * c, x)

    def away(p):
        return (p % 2) * ((p + 1) // 2) + (1 - p % 2) * ((n - p // 2) % n)

    def at_y(k):
        return ((z * n + lax.rem(y + k, n)) * 2 + c, x)

    def at_z(k):
        return ((lax.rem(z + k, n) * n + y) * 2 + c, x)

    def at_x(k):
        return (ep, lax.rem(x + k, NX))

    pending = []
    taken = [0]
    sent = [0]

    class Arrival:
        def __init__(self, ref):
            self.ref, self.sem = ref, taken[0]
            taken[0] += 1
            assert self.sem < rsem.shape[0]

        def wait(self):
            pltpu.make_async_copy(self.ref, self.ref, rsem.at[self.sem]).wait()
            pending.remove(self)

    class Local:
        def __init__(self, src, dst, sem):
            self.made = pltpu.make_async_copy(src, dst, lsem.at[sem])

        def start(self):
            self.made.start()
            pending.append(self)

        def wait(self):
            self.made.wait()
            pending.remove(self)

    def size(ref):
        return math.prod(ref.shape) * ref.dtype.itemsize

    def send(src, dst, arrival, to, times=1):
        pltpu.make_async_remote_copy(
            src_ref=src, dst_ref=dst, send_sem=ssem.at[0], recv_sem=rsem.at[arrival.sem],
            device_id=to, device_id_type=MESH,
        ).start()
        sent[0] += times * size(src)
        if arrival not in pending:
            pending.append(arrival)

    def send_each(low, high, arrival, make):
        if low < high:

            def step(p, carry):
                src, dst, to = make(p)
                send(src, dst, arrival, to, high - low)
                return carry

            lax.fori_loop(low, high, step, 0)

    def finish():
        for one in list(pending):
            one.wait()
        span = tally.at[pl.ds(0, sent[0] // 256)]
        pltpu.make_async_copy(span, span, ssem.at[0]).wait()

    barrier = pltpu.get_barrier_semaphore()

    def greet(k, carry):
        for to in (at_y(k), at_z(k)):
            pl.semaphore_signal(barrier, inc=1, device_id=to, device_id_type=MESH)
        return carry

    lax.fori_loop(1, n, greet, 0)
    for k in range(NX):
        if k:
            pl.semaphore_signal(barrier, inc=1, device_id=at_x(k), device_id_type=MESH)
        pl.semaphore_signal(
            barrier, inc=1, device_id=(sib[0], lax.rem(x + k, NX)), device_id_type=MESH
        )

    moves = (
        (ids_hbm, ids_ref), (gw_hbm, gw_ref), (tok_hbm, tok_ref), (dy_hbm, dy_ref),
        (sg_hbm, sg_ref), (su_hbm, su_ref), (sd_hbm, sd_ref),
        (wg_hbm.at[0], wg), (wu_hbm.at[0], wu), (wd_hbm.at[0], wd),
    )
    loads = [Local(a, b, i) for i, (a, b) in enumerate(moves)]
    for load in loads:
        load.start()
    for load in loads[:4]:
        load.wait()

    ids = ids_ref[...]
    gates = gw_ref[...].astype(F32)
    row = iota((rows, toks), 0)
    slot = row % 2
    outer, inner = away(row // msg), away((row // 2) % n)
    earlier = one_hot(iota((toks, toks), 0) < iota((toks, toks), 1))

    def place(expert):
        named = [ids[k : k + 1] == expert for k in range(top)]
        hits = functools.reduce(jnp.logical_or, named)
        before = dot(one_hot(hits), earlier, 1, 0)
        return named, jnp.logical_and(hits, before == slot.astype(F32))

    named_a, here_a = place(((z + outer) % n) * n + (y + inner) % n)
    named_b, here_b = place(((z + inner) % n) * n + (y + outer) % n)
    weight_b = sum(jnp.where(named_b[k], gates[k : k + 1], 0.0) for k in range(top))
    put_a = one_hot(here_a)
    put_b = jnp.where(here_b, weight_b, 0.0).astype(BF)
    tok = tok_ref[...]
    dy = dy_ref[...]
    pack_a[...] = dot(put_a, tok, 1, 0).astype(BF).reshape(n, msg, feats)
    pack_b[...] = dot(put_b, dy, 1, 0).astype(BF).reshape(n, msg, feats)

    pl.semaphore_wait(barrier, 2 * (n - 1) + 2 * NX - 1)

    others = pl.ds(1, n - 1)
    a1 = Arrival(buf_a.at[others])
    b1 = Arrival(buf_b.at[others])
    send_each(1, n, a1, lambda p: (pack_a.at[p], buf_a.at[p], at_z(away(p))))
    send_each(1, n, b1, lambda p: (pack_b.at[p], buf_b.at[p], at_y(away(p))))

    for load in loads[4:7]:
        load.wait()
    tiles = []
    for block in (sg_ref[...], su_ref[...], sd_ref[...]):
        pad = jnp.zeros((16, TILES // 3 * LANES - shared), BF)
        block = jnp.concatenate([block, pad], axis=1)
        tiles += [block[:, i * LANES : (i + 1) * LANES] for i in range(TILES // 3)]
    for i, tile in enumerate(tiles):
        if i < FIRST:
            g1[y, z, i] = tile
        else:
            g2[z, y, i - FIRST] = tile
    w1 = Arrival(g1.at[0, pl.ds(0, n - 1)])
    w2 = Arrival(g2.at[0, pl.ds(0, n - 1)])

    def send_weights():
        send_each(1, n, w1, lambda p: (g1.at[y, z], g1.at[y, z], at_z(away(p))))
        send_each(1, n, w2, lambda p: (g2.at[z, y], g2.at[z, y], at_y(away(p))))

    send_weights()

    col = iota((feats, feats), 1)
    col_in = col % half
    feature = 32 * (col_in // 16) + 16 * (col // half) + col_in % 16
    sel[...] = one_hot(iota((feats, feats), 0) == feature)
    s_all = dot(jnp.concatenate([tok, dy], axis=0), sel[...], 1, 0).astype(BF)
    s_out[0] = s_all[:, :half]
    s_out[1] = s_all[:, half:]
    sx[c, x] = s_out[c]
    s_same = Arrival(sx.at[0, pl.ds(0, NX - 1)])
    s_other = Arrival(sx.at[0])
    send_each(1, NX, s_same, lambda k: (s_out.at[c], sx.at[c, x], at_x(k)))
    send_each(0, NX, s_other, lambda k: (
        s_out.at[1 - c], sx.at[c, x], (sib[0], lax.rem(x + k, NX))))

    turned_row = iota((rows, rows), 0)
    turned = ((turned_row // 2) % n) * msg + (turned_row // msg) * 2 + turned_row % 2
    turn_f32 = jnp.where(iota((rows, rows), 1) == turned, 1.0, 0.0)
    turn = turn_f32.astype(BF)
    buf_a[0] = pack_a[0]
    buf_b[0] = pack_b[0]

    def part(p):
        return pl.ds(pl.multiple_of(p * msg, msg), msg)

    spans = [pl.ds(low * msg, (high - low) * msg) for low, high in chunks]
    a1.wait()
    mid_a[...] = dot(turn, buf_a[...].reshape(rows, feats), 1, 0).astype(BF).reshape(n, msg, feats)
    a2 = [Arrival(mid_a.at[pl.ds(max(low, 1), high - max(low, 1))]) for low, high in chunks]
    for (low, high), arrival in zip(chunks, a2):
        send_each(max(low, 1), high, arrival, lambda p: (
            mid_a.at[p], rx.at[c, x, part(p)], at_y(away(p))))
    rx[c, x, 0:msg] = mid_a[0]
    b1.wait()
    mid_b[...] = dot(turn, buf_b[...].reshape(rows, feats), 1, 0).astype(BF).reshape(n, msg, feats)
    b2 = [Arrival(mid_b.at[pl.ds(max(low, 1), high - max(low, 1))]) for low, high in chunks]
    for (low, high), arrival in zip(chunks, b2):
        send_each(max(low, 1), high, arrival, lambda p: (
            mid_b.at[p], rd.at[c, x, part(p)], at_z(away(p))))
    rd[c, x, 0:msg] = mid_b[0]

    class Ring:
        def __init__(self, buf, pos, go):
            self.buf, self.pos, self.go, self.step = buf, pos, go, 0
            self.flying = []

        def block(self, k):
            return lax.rem(self.pos + k + 2 * n, n)

        def forward(self):
            for arrival in self.flying:
                arrival.wait()
            self.flying = []
            s, last = self.step, n // 2 - 1
            if s <= last:
                if s < last:
                    arrival = Arrival(self.buf.at[pl.ds(0, 2)])
                else:
                    arrival = Arrival(self.buf.at[0])
                self.flying.append(arrival)
                for way in (1, -1):
                    at = self.buf.at[self.block(-way * s)]
                    if s == last:
                        at = at.at[pl.ds(0, n // 2) if way == 1 else pl.ds(n // 2, n // 2)]
                    send(at, at, arrival, self.go(way % n))
            self.step += 1

    ring1 = Ring(g1, y, at_y)
    ring2 = Ring(g2, z, at_z)

    def rings():
        ring1.forward()
        ring2.forward()

    def rings_first():
        w1.wait()
        ring1.forward()
        w2.wait()
        ring2.forward()

    left, right = lax.rem(x + NX - 1, NX), lax.rem(x + 1, NX)
    two = pl.ds(0, 2)
    sib_rows = [Arrival(rx.at[0, two]) for _ in range(NX)]

    def to_x(buf, at, h, k):
        ref = buf.at[c, at, spans[h]]
        arrival = Arrival(ref)
        send(ref, ref, arrival, at_x(k % NX))
        return arrival

    def to_sib(buf, k, h):
        ref = buf.at[c, lax.rem(x + k, NX), spans[h]]
        send(ref, ref, sib_rows[k], sib)

    x_right, x_left, d_right, d_left = [], [], [], []
    for h in range(len(chunks)):
        a2[h].wait()
        x_right.append(to_x(rx, x, h, 1))
        x_left.append(to_x(rx, x, h, -1))
        to_sib(rx, 0, h)
        b2[h].wait()
        d_left.append(to_x(rd, x, h, -1))
        d_right.append(to_x(rd, x, h, 1))
        to_sib(rd, 0, h)
        if h == 1:
            rings_first()

    x_on, d_on = [], []
    for h in range(len(chunks)):
        x_right[h].wait()
        x_on.append(to_x(rx, left, h, 1))
        to_sib(rx, 3, h)
        d_left[h].wait()
        d_on.append(to_x(rd, right, h, -1))
        to_sib(rd, 1, h)
        x_left[h].wait()
        to_sib(rx, 1, h)
        d_right[h].wait()
        to_sib(rd, 3, h)
    rings()

    for load in loads[7:]:
        load.wait()

    def quarter(ref, q):
        return jnp.concatenate([ref[0, q], ref[1, q]], axis=0)

    def at_quarter(q):
        return pl.ds(pl.multiple_of(q * feats, feats), feats)

    def w_quarter(q):
        return jnp.concatenate([wg[at_quarter(q)], wu[at_quarter(q)]], axis=1)

    pre = jnp.zeros((2 * rows, 2 * hid), F32)
    q_back = jnp.zeros((2 * rows, hid), F32)
    for k in (0, 1, 3, 2):
        if k == 2:
            for h in range(len(chunks)):
                x_on[h].wait()
                to_sib(rx, 2, h)
                d_on[h].wait()
                to_sib(rd, 2, h)
        sib_rows[k].wait()
        q = lax.rem(x + k, NX)
        pre = pre + dot(quarter(rx, q), w_quarter(q), 1, 0)
        q_back = q_back + dot(quarter(rd, q), wd[:, at_quarter(q)], 1, 1)

    def both_halves(f, a):
        return jnp.concatenate([f(a[:rows]), f(a[rows:])], axis=0)

    q_back = both_halves(
        lambda a: dot(turn_f32, a, 1, 0, precision=lax.Precision.HIGHEST), q_back
    )

    def silu_parts(pre_gate, pre_up, back):
        sigma = jax.nn.sigmoid(pre_gate)
        active = pre_gate * sigma
        d_gate = back * pre_up * sigma * (1.0 + pre_gate * (1.0 - sigma))
        return active * pre_up, jnp.concatenate([d_gate, back * active], axis=1).astype(BF)

    hidden, d_both = silu_parts(pre[:, :hid], pre[:, hid:], q_back)
    router = jnp.sum(hidden * q_back, axis=1, keepdims=True)
    hidden = both_halves(lambda a: dot(turn, a, 1, 0).astype(BF), hidden.astype(BF))

    first_half = c == 0
    d_own = jnp.where(first_half, d_both[:rows], d_both[rows:])
    d_sibs = jnp.where(first_half, d_both[rows:], d_both[:rows])
    r_own = jnp.where(first_half, router[:rows], router[rows:])
    r_sibs = jnp.where(first_half, router[rows:], router[:rows])

    def coded(value, at):
        first = value.astype(BF).astype(F32)
        return jnp.where(at == 0, first, jnp.where(at == 1, value - first, 0.0)).astype(BF)

    def as_row(column):
        return jnp.broadcast_to(column, (rows, 16)).T

    def row_sum(tile):
        return jnp.sum(tile.astype(F32), axis=0, keepdims=True)

    tile_row = iota((16, rows), 0)
    rt_out[...] = coded(as_row(r_sibs), tile_row)
    router_sib = Arrival(rt_in)
    send(rt_out, rt_in, router_sib, sib)
    part_sib = []
    for k in range(NX):
        sib_out[k] = dot(d_sibs, w_quarter(lax.rem(x + k, NX)), 1, 1).astype(BF)
        part_sib.append(Arrival(sib_in.at[k]))
        send(sib_out.at[k], sib_in.at[k], part_sib[k], sib)
    own = [dot(d_own, w_quarter(lax.rem(x + k, NX)), 1, 1) for k in range(NX)]
    router_sib.wait()
    r_chip = as_row(r_own) + row_sum(rt_in[...])
    rr_out[...] = coded(r_chip, tile_row)
    router_rs = Arrival(rr_in.at[pl.ds(1, NX - 1)])
    send_each(1, NX, router_rs, lambda k: (rr_out, rr_in.at[k], at_x(k)))
    for k in range(NX):
        part_sib[k].wait()
        rs_out[k] = (own[k] + sib_in[k].astype(F32)).astype(BF)
    rs = {}
    for h in reversed(range(len(chunks))):
        rs[h] = Arrival(rs_in.at[pl.ds(1, NX - 1), spans[h]])
        for k in (2, 1, 3):
            send(rs_out.at[k, spans[h]], rs_in.at[k, spans[h]], rs[h], at_x(k))
    rings()

    for q in range(NX):
        span = slice(q * feats, (q + 1) * feats)
        both = dot(quarter(rx, q), d_both, 0, 0).astype(BF)
        ggrad[0, span] = both[:, :hid]
        ugrad[0, span] = both[:, hid:]
        dgrad[0, :, span] = dot(hidden, quarter(rd, q), 0, 0).astype(BF)
    stores = [
        Local(a, b, len(loads) + i)
        for i, (a, b) in enumerate((
            (gt_ref, gt_hbm), (gg_ref, gg_hbm),
            (ggrad, ggrad_hbm), (ugrad, ugrad_hbm), (dgrad, dgrad_hbm),
        ))
    ]
    for store in stores[2:]:
        store.start()

    router_rs.wait()
    r_all = row_sum(rr_out[...])
    for k in range(1, NX):
        r_all = r_all + row_sum(rr_in[k])
    r_total = coded(jnp.broadcast_to(r_all, (LANES, rows)).T, iota((rows, LANES), 1))
    back_1 = Arrival(ret_1.at[others])
    for h in reversed(range(len(chunks))):
        low, high = chunks[h]
        rs[h].wait()
        total = rs_out[0, spans[h]].astype(F32)
        for k in range(1, NX):
            total = total + rs_in[k, spans[h]].astype(F32)
        r_part = r_total[low * msg : high * msg]
        block = jnp.concatenate([total.astype(BF), r_part], axis=1)
        ret_out[low:high] = block.reshape(high - low, msg, feats + LANES)
        send_each(max(low, 1), high, back_1, lambda p: (
            ret_out.at[p], ret_1.at[p], at_y(n - away(p))))
    ret_1[0] = ret_out[0]
    rings()

    def weights(i):
        if i < FIRST:
            parts = [g1[:, k, i].reshape(n * 16, LANES) for k in range(n)]
        else:
            parts = [g2[k, :, i - FIRST].reshape(n * 16, LANES) for k in range(n)]
        return jnp.concatenate(parts, axis=0)

    def matrix(m):
        return jnp.concatenate([weights(3 * m + i) for i in range(3)], axis=1)

    def features(low):
        return jnp.concatenate(
            [
                jnp.concatenate([sx[s, q, low : low + toks] for q in range(NX)], axis=1)
                for s in range(2)
            ],
            axis=0,
        )

    width = 3 * LANES

    def shared_one():
        s_same.wait()
        s_other.wait()
        s_tok = features(0)
        pre_out[:, :width] = dot(s_tok, matrix(0), 1, 0)
        pre_out[:, width : 2 * width] = dot(s_tok, matrix(1), 1, 0)
        pre_out[:, 2 * width :] = dot(features(toks), matrix(2), 1, 0)
        arrival = Arrival(pre_in)
        send(pre_out, pre_in, arrival, sib)
        return arrival


    back_1.wait()
    wide = feats + LANES
    ret_mid[...] = dot(turn, ret_1[...].reshape(rows, wide), 1, 0).astype(BF).reshape(n, msg, wide)
    back_2 = Arrival(ret_2.at[others])
    send_each(1, n, back_2, lambda p: (ret_mid.at[p], ret_2.at[p], at_z(n - away(p))))
    ret_2[0] = ret_mid[0]
    rings()
    pre_sib = shared_one()

    pre_sib.wait()
    s_pre = pre_out[...] + pre_in[...]
    _, s_both = silu_parts(s_pre[:, :width], s_pre[:, width : 2 * width], s_pre[:, 2 * width :])
    piece = dot(s_both[:, :width], matrix(0), 1, 1) + dot(s_both[:, width:], matrix(1), 1, 1)
    for q in range(NX):
        piece_out[q] = piece[:, q * half : (q + 1) * half].astype(BF)
    s_rs = Arrival(piece_in.at[pl.ds(1, NX - 1)])
    send_each(1, NX, s_rs, lambda k: (
        piece_out.at[lax.rem(x + k, NX)], piece_in.at[k], at_x(k)))
    s_rs.wait()
    s_sum = piece_out[x].astype(F32)
    for k in range(1, NX):
        s_sum = s_sum + piece_in[k].astype(F32)
    s_sum = s_sum.astype(BF)
    s_own = jnp.where(first_half, s_sum[:toks], s_sum[toks:])
    fx_out[...] = jnp.where(first_half, s_sum[toks:], s_sum[:toks])
    s_fx = Arrival(fx_in)
    send(fx_out, fx_in, s_fx, sib)

    back_2.wait()
    came = ret_2[...].reshape(rows, wide)
    routed = dot(put_a, came[:, :feats], 0, 0)
    routers = jnp.sum(came[:, feats:].astype(F32), axis=1, keepdims=True)
    gg_ref[...] = jnp.concatenate(
        [
            jnp.sum(
                jnp.where(jnp.logical_and(here_a, named_a[k]), routers, 0.0),
                axis=0, keepdims=True,
            )
            for k in range(top)
        ],
        axis=0,
    ) / gates
    stores[1].start()
    s_fx.wait()
    s_other_half = fx_in[...]
    both = jnp.concatenate(
        [
            jnp.where(first_half, s_own, s_other_half),
            jnp.where(first_half, s_other_half, s_own),
        ],
        axis=1,
    )
    gt_ref[...] = (routed + dot(both, sel[...], 1, 1)).astype(BF)
    stores[0].start()
    finish()


def hand_out(*refs):
    count = (len(refs) - 2) // 3
    ins, outs, held = refs[:count], refs[count : 2 * count], refs[2 * count : 3 * count]
    fetch, store = refs[3 * count :]
    reads = [pltpu.make_async_copy(ins[i], held[i], fetch.at[i]) for i in range(count)]
    writes = [pltpu.make_async_copy(held[i], outs[i], store.at[i]) for i in range(count)]
    for read in reads:
        read.start()
    for read, write in zip(reads, writes):
        read.wait()
        write.start()
    for write in writes:
        write.wait()


def body(tokens, out_grad, gate_weights, expert_ids, w_gate, w_up, w_down, s_gate, s_up, s_down):
    n = round((lax.axis_size("ep") // 2) ** 0.5)
    toks, feats = tokens.shape
    hid = w_gate.shape[2]
    rows, msg, half = 2 * n * n, 2 * n, feats // 2
    vmem = pl.BlockSpec(memory_space=pltpu.VMEM)
    hbm = pl.BlockSpec(memory_space=pltpu.HBM)

    def legs(lanes, count):
        return [pltpu.VMEM((n, msg, lanes), BF) for _ in range(count)]

    def like(a):
        return jax.ShapeDtypeStruct(a.shape, a.dtype)

    arrays = (
        tokens, out_grad, gate_weights.T, expert_ids.T, w_gate, w_up, w_down,
        s_gate, s_up, s_down.T,
    )
    results = (
        like(tokens),
        jax.ShapeDtypeStruct(gate_weights.shape[::-1], F32),
        like(w_gate),
        like(w_up),
        like(w_down),
    )
    scratch = (
        [pltpu.VMEM(a.shape, a.dtype) for a in results]
        + [pltpu.VMEM(arrays[i].shape, arrays[i].dtype) for i in (0, 1, 2, 3, 7, 8, 9)]
        + legs(feats, 6)
        + [pltpu.VMEM((2, NX, rows, feats), BF)] * 2
        + [pltpu.VMEM(a.shape[1:], BF) for a in (w_gate, w_up, w_down)]
        + [pltpu.VMEM((NX, rows, feats), BF)] * 4
        + [pltpu.VMEM((16, rows), BF)] * 3
        + [pltpu.VMEM((NX, 16, rows), BF)]
        + legs(feats + LANES, 4)
        + [
            pltpu.VMEM((feats, feats), BF),
            pltpu.VMEM((2, 2 * toks, half), BF),
            pltpu.VMEM((2, NX, 2 * toks, half), BF),
            pltpu.VMEM((n, n, FIRST, 16, LANES), BF),
            pltpu.VMEM((n, n, TILES - FIRST, 16, LANES), BF),
            pltpu.VMEM((2 * toks, TILES * LANES), F32),
            pltpu.VMEM((2 * toks, TILES * LANES), F32),
            pltpu.VMEM((NX, 2 * toks, half), BF),
            pltpu.VMEM((NX, 2 * toks, half), BF),
            pltpu.VMEM((toks, half), BF),
            pltpu.VMEM((toks, half), BF),
            pltpu.VMEM((32768, LANES), BF),
            pltpu.SemaphoreType.DMA((1,)),
            pltpu.SemaphoreType.DMA((76,)),
            pltpu.SemaphoreType.DMA((len(arrays) + len(results),)),
        ]
    )
    made = pl.pallas_call(
        functools.partial(kernel, n),
        out_shape=results,
        in_specs=[hbm] * len(arrays),
        out_specs=(hbm,) * len(results),
        scratch_shapes=scratch,
        compiler_params=pltpu.CompilerParams(
            collective_id=0, has_side_effects=True, vmem_limit_bytes=LIMIT
        ),
    )(*arrays)
    given = pl.pallas_call(
        hand_out,
        out_shape=results,
        in_specs=[hbm] * len(results),
        out_specs=(hbm,) * len(results),
        scratch_shapes=[pltpu.VMEM(a.shape, a.dtype) for a in results]
        + [pltpu.SemaphoreType.DMA((len(results),))] * 2,
        compiler_params=pltpu.CompilerParams(vmem_limit_bytes=LIMIT),
    )(*made)
    return (given[0], given[1].T) + tuple(given[2:])


def solution(mesh):
    placed = (
        P("ep", "tp"),
        P("ep", "tp"),
        P("ep", None),
        P("ep", None),
        P("ep", None, "tp"),
        P("ep", None, "tp"),
        P("ep", "tp", None),
        P("ep", "tp"),
        P("ep", "tp"),
        P("tp", "ep"),
    )
    return jax.shard_map(
        body,
        mesh=mesh,
        in_specs=placed,
        out_specs=(
            P("ep", "tp"),
            P("ep", None),
            P("ep", None, "tp"),
            P("ep", None, "tp"),
            P("ep", "tp", None),
        ),
        check_vma=False,
    )
```

time: 78.6 us -> 63.6 us (0.81)
  local copies, waits for them, and re-layouts: 9.06 us -> 0 us
  Pallas kernels: 68.5 us -> 62.7 us
    unnamed x23 -> x0, local copies, waits for them, and re-layouts: 8.39 us -> none
    pallas_call x1 -> x2, Pallas kernels: 68.5 us -> 62.7 us  [the longest x1 60.4 us: body(): pl.pallas_call(functools.partial(kernel, n), out_shape=results, in_specs=...]
where the time goes in v2:
time: 63.6 us; the launch traced here: 63.4 us
  Pallas kernels  62.7 us (99%)
  between operations  0.64 us (1%)
    pallas_call x1, Pallas kernels, body(): pl.pallas_call(functools.partial(kernel, n), out_shape=results, in_specs=...  60.4 us
    pallas_call x1, Pallas kernels, body(): pl.pallas_call(hand_out, out_shape=results, in_specs=[hbm] * len(results)...  2.29 us

profile of v2, /device:TPU:1, one launch (start us, length us, event | category | flops | bytes accessed | tf_op | source)
XLA Modules:
  0.0 63.4 jit_solution(284995699578837056)
XLA Ops:
  0.6 60.4 %shard_map.137 = (bf16[16,512]{1,0:T(8,128)(2,1)}, f32[6,16]{1,0:T(8,128)}, bf16[1,2048,128]{2,1,0:T(8,128)(2,1)}, bf16[1,2048,128]{2,1,0:T(8,128)(2,1)}, bf16[1,128,2048]{2,1,0:T(8,128)(2,1)}) custom-call(bf16[16,512]{1,0:T(8,128)(2,1)} %tok_hbm.1, bf16[16,512]{1,0:T(8,128)(2,1)} %dy_hbm.1, bf16[6,16]{1,0:T(8,128)(2,1)} %bitcast.6, s32[6,16]{1,0:T(8,128)} %bitcast.5, ...), custom_call_target="tpu_custom_call" | custom-call | tf_op jit(solution)/shard_map/pallas_call | solution.py:602
  61.1 2.3 %shard_map.138 = (bf16[16,512]{1,0:T(8,128)(2,1)}, f32[6,16]{1,0:T(8,128)}, bf16[1,2048,128]{2,1,0:T(8,128)(2,1)}, bf16[1,2048,128]{2,1,0:T(8,128)(2,1)}, bf16[1,128,2048]{2,1,0:T(8,128)(2,1)}) custom-call(bf16[16,512]{1,0:T(8,128)(2,1)} %get-tuple-element.15.refs_0_, f32[6,16]{1,0:T(8,128)} %get-tuple-element.16.refs_1_, ...), custom_call_target="tpu_custom_call" | custom-call | tf_op jit(solution)/shard_map/pallas_call | solution.py:612

commit v3 on v2

--- a/solution.py
+++ b/solution.py
@@ -36,7 +36,7 @@
     gt_hbm, gg_hbm, ggrad_hbm, ugrad_hbm, dgrad_hbm,
     gt_ref, gg_ref, ggrad, ugrad, dgrad, tok_ref, dy_ref, gw_ref, ids_ref, sg_ref, su_ref, sd_ref,
     pack_a, pack_b, buf_a, buf_b, mid_a, mid_b, rx, rd, wg, wu, wd,
-    sib_out, sib_in, rs_out, rs_in, rt_out, rt_in, rr_out, rr_in, ret_out, ret_1, ret_mid, ret_2,
+    rs_out, rs_in, rr_out, rr_in, dd_out, dd, ret_out, ret_1, ret_mid, ret_2,
     sel, s_out, sx, g1, g2, pre_out, pre_in, piece_out, piece_in, fx_out, fx_in, tally,
     ssem, rsem, lsem,
 ):
@@ -110,8 +110,8 @@
     def send_each(low, high, arrival, make):
         if low < high:
 
-            def step(p, carry):
-                src, dst, to = make(p)
+            def step(i, carry):
+                src, dst, to = make(low + high - 1 - i)
                 send(src, dst, arrival, to, high - low)
                 return carry
 
@@ -141,7 +141,7 @@
     moves = (
         (ids_hbm, ids_ref), (gw_hbm, gw_ref), (tok_hbm, tok_ref), (dy_hbm, dy_ref),
         (sg_hbm, sg_ref), (su_hbm, su_ref), (sd_hbm, sd_ref),
-        (wg_hbm.at[0], wg), (wu_hbm.at[0], wu), (wd_hbm.at[0], wd),
+        (wg_hbm.at[0], wg.at[c]), (wu_hbm.at[0], wu.at[c]), (wd_hbm.at[0], wd.at[c]),
     )
     loads = [Local(a, b, i) for i, (a, b) in enumerate(moves)]
     for load in loads:
@@ -214,6 +214,12 @@
     send_each(1, NX, s_same, lambda k: (s_out.at[c], sx.at[c, x], at_x(k)))
     send_each(0, NX, s_other, lambda k: (
         s_out.at[1 - c], sx.at[c, x], (sib[0], lax.rem(x + k, NX))))
+
+    w_sib = []
+    for load, ref in zip(loads[7:], (wg, wu, wd)):
+        load.wait()
+        w_sib.append(Arrival(ref.at[0]))
+        send(ref.at[c], ref.at[c], w_sib[-1], sib)
 
     turned_row = iota((rows, rows), 0)
     turned = ((turned_row // 2) % n) * msg + (turned_row // msg) * 2 + turned_row % 2
@@ -281,8 +287,6 @@
         ring2.forward()
 
     left, right = lax.rem(x + NX - 1, NX), lax.rem(x + 1, NX)
-    two = pl.ds(0, 2)
-    sib_rows = [Arrival(rx.at[0, two]) for _ in range(NX)]
 
     def to_x(buf, at, h, k):
         ref = buf.at[c, at, spans[h]]
@@ -290,20 +294,14 @@
         send(ref, ref, arrival, at_x(k % NX))
         return arrival
 
-    def to_sib(buf, k, h):
-        ref = buf.at[c, lax.rem(x + k, NX), spans[h]]
-        send(ref, ref, sib_rows[k], sib)
-
     x_right, x_left, d_right, d_left = [], [], [], []
     for h in range(len(chunks)):
         a2[h].wait()
         x_right.append(to_x(rx, x, h, 1))
-        x_left.append(to_x(rx, x, h, -1))
-        to_sib(rx, 0, h)
         b2[h].wait()
         d_left.append(to_x(rd, x, h, -1))
+        x_left.append(to_x(rx, x, h, -1))
         d_right.append(to_x(rd, x, h, 1))
-        to_sib(rd, 0, h)
         if h == 1:
             rings_first()
 
@@ -311,48 +309,41 @@
     for h in range(len(chunks)):
         x_right[h].wait()
         x_on.append(to_x(rx, left, h, 1))
-        to_sib(rx, 3, h)
         d_left[h].wait()
         d_on.append(to_x(rd, right, h, -1))
-        to_sib(rd, 1, h)
-        x_left[h].wait()
-        to_sib(rx, 1, h)
-        d_right[h].wait()
-        to_sib(rd, 3, h)
     rings()
 
-    for load in loads[7:]:
-        load.wait()
-
-    def quarter(ref, q):
-        return jnp.concatenate([ref[0, q], ref[1, q]], axis=0)
+    for arrival in w_sib:
+        arrival.wait()
 
     def at_quarter(q):
         return pl.ds(pl.multiple_of(q * feats, feats), feats)
 
     def w_quarter(q):
-        return jnp.concatenate([wg[at_quarter(q)], wu[at_quarter(q)]], axis=1)
-
-    pre = jnp.zeros((2 * rows, 2 * hid), F32)
-    q_back = jnp.zeros((2 * rows, hid), F32)
+        return jnp.concatenate(
+            [ref[u, at_quarter(q)] for ref in (wg, wu) for u in range(2)], axis=1
+        )
+
+    def down_quarter(q):
+        return jnp.concatenate([wd[u, :, at_quarter(q)] for u in range(2)], axis=0)
+
+    both = 2 * hid
+    pre = jnp.zeros((rows, 2 * both), F32)
+    q_back = jnp.zeros((rows, both), F32)
     for k in (0, 1, 3, 2):
+        if k == 1:
+            for arrival in x_left:
+                arrival.wait()
+        if k == 3:
+            for arrival in d_right:
+                arrival.wait()
         if k == 2:
-            for h in range(len(chunks)):
-                x_on[h].wait()
-                to_sib(rx, 2, h)
-                d_on[h].wait()
-                to_sib(rd, 2, h)
-        sib_rows[k].wait()
+            for arrival in x_on + d_on:
+                arrival.wait()
         q = lax.rem(x + k, NX)
-        pre = pre + dot(quarter(rx, q), w_quarter(q), 1, 0)
-        q_back = q_back + dot(quarter(rd, q), wd[:, at_quarter(q)], 1, 1)
-
-    def both_halves(f, a):
-        return jnp.concatenate([f(a[:rows]), f(a[rows:])], axis=0)
-
-    q_back = both_halves(
-        lambda a: dot(turn_f32, a, 1, 0, precision=lax.Precision.HIGHEST), q_back
-    )
+        pre = pre + dot(rx[c, q], w_quarter(q), 1, 0)
+        q_back = q_back + dot(rd[c, q], down_quarter(q), 1, 1)
+    q_back = dot(turn_f32, q_back, 1, 0, precision=lax.Precision.HIGHEST)
 
     def silu_parts(pre_gate, pre_up, back):
         sigma = jax.nn.sigmoid(pre_gate)
@@ -360,15 +351,8 @@
         d_gate = back * pre_up * sigma * (1.0 + pre_gate * (1.0 - sigma))
         return active * pre_up, jnp.concatenate([d_gate, back * active], axis=1).astype(BF)
 
-    hidden, d_both = silu_parts(pre[:, :hid], pre[:, hid:], q_back)
+    hidden, d_both = silu_parts(pre[:, :both], pre[:, both:], q_back)
     router = jnp.sum(hidden * q_back, axis=1, keepdims=True)
-    hidden = both_halves(lambda a: dot(turn, a, 1, 0).astype(BF), hidden.astype(BF))
-
-    first_half = c == 0
-    d_own = jnp.where(first_half, d_both[:rows], d_both[rows:])
-    d_sibs = jnp.where(first_half, d_both[rows:], d_both[:rows])
-    r_own = jnp.where(first_half, router[:rows], router[rows:])
-    r_sibs = jnp.where(first_half, router[rows:], router[:rows])
 
     def coded(value, at):
         first = value.astype(BF).astype(F32)
@@ -381,23 +365,11 @@
         return jnp.sum(tile.astype(F32), axis=0, keepdims=True)
 
     tile_row = iota((16, rows), 0)
-    rt_out[...] = coded(as_row(r_sibs), tile_row)
-    router_sib = Arrival(rt_in)
-    send(rt_out, rt_in, router_sib, sib)
-    part_sib = []
-    for k in range(NX):
-        sib_out[k] = dot(d_sibs, w_quarter(lax.rem(x + k, NX)), 1, 1).astype(BF)
-        part_sib.append(Arrival(sib_in.at[k]))
-        send(sib_out.at[k], sib_in.at[k], part_sib[k], sib)
-    own = [dot(d_own, w_quarter(lax.rem(x + k, NX)), 1, 1) for k in range(NX)]
-    router_sib.wait()
-    r_chip = as_row(r_own) + row_sum(rt_in[...])
-    rr_out[...] = coded(r_chip, tile_row)
+    rr_out[...] = coded(as_row(router), tile_row)
     router_rs = Arrival(rr_in.at[pl.ds(1, NX - 1)])
     send_each(1, NX, router_rs, lambda k: (rr_out, rr_in.at[k], at_x(k)))
-    for k in range(NX):
-        part_sib[k].wait()
-        rs_out[k] = (own[k] + sib_in[k].astype(F32)).astype(BF)
+    for k in (2, 1, 3, 0):
+        rs_out[k] = dot(d_both, w_quarter(lax.rem(x + k, NX)), 1, 1).astype(BF)
     rs = {}
     for h in reversed(range(len(chunks))):
         rs[h] = Arrival(rs_in.at[pl.ds(1, NX - 1), spans[h]])
@@ -405,12 +377,21 @@
             send(rs_out.at[k, spans[h]], rs_in.at[k, spans[h]], rs[h], at_x(k))
     rings()
 
-    for q in range(NX):
-        span = slice(q * feats, (q + 1) * feats)
-        both = dot(quarter(rx, q), d_both, 0, 0).astype(BF)
-        ggrad[0, span] = both[:, :hid]
-        ugrad[0, span] = both[:, hid:]
-        dgrad[0, :, span] = dot(hidden, quarter(rd, q), 0, 0).astype(BF)
+    first_half = c == 0
+    hidden = dot(turn, hidden.astype(BF), 1, 0).astype(BF)
+    parts = [
+        jnp.concatenate(
+            [a[:, u * hid : (u + 1) * hid] for a in (d_both[:, :both], d_both[:, both:], hidden)],
+            axis=1,
+        )
+        for u in range(2)
+    ]
+    dd[c] = jnp.where(first_half, parts[0], parts[1])
+    dd_out[...] = jnp.where(first_half, parts[1], parts[0])
+    dd_sib, x_sib, d_sib = Arrival(dd.at[0]), Arrival(rx.at[0]), Arrival(rd.at[0])
+    send(dd_out, dd.at[c], dd_sib, sib)
+    send(rx.at[c], rx.at[c], x_sib, sib)
+    send(rd.at[c], rd.at[c], d_sib, sib)
     stores = [
         Local(a, b, len(loads) + i)
         for i, (a, b) in enumerate((
@@ -418,8 +399,22 @@
             (ggrad, ggrad_hbm), (ugrad, ugrad_hbm), (dgrad, dgrad_hbm),
         ))
     ]
-    for store in stores[2:]:
-        store.start()
+
+    def weight_gradients():
+        for arrival in (dd_sib, x_sib, d_sib):
+            arrival.wait()
+        parts = jnp.concatenate([dd[0], dd[1]], axis=0)
+        for q in range(NX):
+            span = slice(q * feats, (q + 1) * feats)
+            rows_x = jnp.concatenate([rx[0, q], rx[1, q]], axis=0)
+            rows_d = jnp.concatenate([rd[0, q], rd[1, q]], axis=0)
+            grads = dot(rows_x, parts[:, : 2 * hid], 0, 0).astype(BF)
+            ggrad[0, span] = grads[:, :hid]
+            ugrad[0, span] = grads[:, hid:]
+            dgrad[0, :, span] = dot(parts[:, 2 * hid :], rows_d, 0, 0).astype(BF)
+        for store in stores[2:]:
+            store.start()
+
 
     router_rs.wait()
     r_all = row_sum(rr_out[...])
@@ -439,6 +434,7 @@
         send_each(max(low, 1), high, back_1, lambda p: (
             ret_out.at[p], ret_1.at[p], at_y(n - away(p))))
     ret_1[0] = ret_out[0]
+    weight_gradients()
     rings()
 
     def weights(i):
@@ -519,14 +515,14 @@
     stores[1].start()
     s_fx.wait()
     s_other_half = fx_in[...]
-    both = jnp.concatenate(
+    s_both = jnp.concatenate(
         [
             jnp.where(first_half, s_own, s_other_half),
             jnp.where(first_half, s_other_half, s_own),
         ],
         axis=1,
     )
-    gt_ref[...] = (routed + dot(both, sel[...], 1, 1)).astype(BF)
+    gt_ref[...] = (routed + dot(s_both, sel[...], 1, 1)).astype(BF)
     stores[0].start()
     finish()
 
@@ -576,10 +572,10 @@
         + [pltpu.VMEM(arrays[i].shape, arrays[i].dtype) for i in (0, 1, 2, 3, 7, 8, 9)]
         + legs(feats, 6)
         + [pltpu.VMEM((2, NX, rows, feats), BF)] * 2
-        + [pltpu.VMEM(a.shape[1:], BF) for a in (w_gate, w_up, w_down)]
-        + [pltpu.VMEM((NX, rows, feats), BF)] * 4
-        + [pltpu.VMEM((16, rows), BF)] * 3
-        + [pltpu.VMEM((NX, 16, rows), BF)]
+        + [pltpu.VMEM((2,) + a.shape[1:], BF) for a in (w_gate, w_up, w_down)]
+        + [pltpu.VMEM((NX, rows, feats), BF)] * 2
+        + [pltpu.VMEM((16, rows), BF), pltpu.VMEM((NX, 16, rows), BF)]
+        + [pltpu.VMEM((rows, 3 * hid), BF), pltpu.VMEM((2, rows, 3 * hid), BF)]
         + legs(feats + LANES, 4)
         + [
             pltpu.VMEM((feats, feats), BF),

time: 63.6 us -> 59.6 us (0.937)
  Pallas kernels: 62.7 us -> 58.7 us
    pallas_call x1, Pallas kernels: 60.4 us -> 56.4 us  [body(): pl.pallas_call(functools.partial(kernel, n), out_shape=results, in_specs=...]
where the time goes in v3:
time: 59.6 us; the launch traced here: 59.3 us
  Pallas kernels  58.7 us (98%)
  between operations  0.64 us (1%)
    pallas_call x1, Pallas kernels, body(): pl.pallas_call(functools.partial(kernel, n), out_shape=results, in_specs=...  56.4 us
    pallas_call x1, Pallas kernels, body(): pl.pallas_call(hand_out, out_shape=results, in_specs=[hbm] * len(results)...  2.29 us

profile of v3, /device:TPU:1, one launch (start us, length us, event | category | flops | bytes accessed | tf_op | source)
XLA Modules:
  0.0 59.3 jit_solution(17672135605652922001)
XLA Ops:
  0.6 56.4 %shard_map.137 = (bf16[16,512]{1,0:T(8,128)(2,1)}, f32[6,16]{1,0:T(8,128)}, bf16[1,2048,128]{2,1,0:T(8,128)(2,1)}, bf16[1,2048,128]{2,1,0:T(8,128)(2,1)}, bf16[1,128,2048]{2,1,0:T(8,128)(2,1)}) custom-call(bf16[16,512]{1,0:T(8,128)(2,1)} %tok_hbm.1, bf16[16,512]{1,0:T(8,128)(2,1)} %dy_hbm.1, bf16[6,16]{1,0:T(8,128)(2,1)} %bitcast.6, s32[6,16]{1,0:T(8,128)} %bitcast.5, ...), custom_call_target="tpu_custom_call" | custom-call | tf_op jit(solution)/shard_map/pallas_call | solution.py:598
  57.0 2.3 %shard_map.138 = (bf16[16,512]{1,0:T(8,128)(2,1)}, f32[6,16]{1,0:T(8,128)}, bf16[1,2048,128]{2,1,0:T(8,128)(2,1)}, bf16[1,2048,128]{2,1,0:T(8,128)(2,1)}, bf16[1,128,2048]{2,1,0:T(8,128)(2,1)}) custom-call(bf16[16,512]{1,0:T(8,128)(2,1)} %get-tuple-element.15.refs_0_, f32[6,16]{1,0:T(8,128)} %get-tuple-element.16.refs_1_, ...), custom_call_target="tpu_custom_call" | custom-call | tf_op jit(solution)/shard_map/pallas_call | solution.py:608

commit v4 on v3

--- a/solution.py
+++ b/solution.py
@@ -49,6 +49,8 @@
     top = ids_ref.shape[0]
     edges = sorted({0, min(3, n), min(5, n), n})
     chunks = list(zip(edges, edges[1:]))
+    near = sorted({0, 1, min(3, n), min(5, n), n})
+    near_chunks = list(zip(near, near[1:]))
 
     ep = lax.axis_index("ep")
     x = lax.axis_index("tp")
@@ -123,28 +125,26 @@
         span = tally.at[pl.ds(0, sent[0] // 256)]
         pltpu.make_async_copy(span, span, ssem.at[0]).wait()
 
-    barrier = pltpu.get_barrier_semaphore()
-
-    def greet(k, carry):
-        for to in (at_y(k), at_z(k)):
-            pl.semaphore_signal(barrier, inc=1, device_id=to, device_id_type=MESH)
-        return carry
-
-    lax.fori_loop(1, n, greet, 0)
-    for k in range(NX):
-        if k:
-            pl.semaphore_signal(barrier, inc=1, device_id=at_x(k), device_id_type=MESH)
-        pl.semaphore_signal(
-            barrier, inc=1, device_id=(sib[0], lax.rem(x + k, NX)), device_id_type=MESH
-        )
-
     moves = (
         (ids_hbm, ids_ref), (gw_hbm, gw_ref), (tok_hbm, tok_ref), (dy_hbm, dy_ref),
         (sg_hbm, sg_ref), (su_hbm, su_ref), (sd_hbm, sd_ref),
         (wg_hbm.at[0], wg.at[c]), (wu_hbm.at[0], wu.at[c]), (wd_hbm.at[0], wd.at[c]),
     )
     loads = [Local(a, b, i) for i, (a, b) in enumerate(moves)]
-    for load in loads:
+    for load in loads[:4]:
+        load.start()
+
+    barrier = pltpu.get_barrier_semaphore()
+    for p in reversed(range(1, n)):
+        for to in (at_y(away(p)), at_z(away(p))):
+            pl.semaphore_signal(barrier, inc=1, device_id=to, device_id_type=MESH)
+    for k in reversed(range(NX)):
+        if k:
+            pl.semaphore_signal(barrier, inc=1, device_id=at_x(k), device_id_type=MESH)
+        pl.semaphore_signal(
+            barrier, inc=1, device_id=(sib[0], lax.rem(x + k, NX)), device_id_type=MESH
+        )
+    for load in loads[4:]:
         load.start()
     for load in loads[:4]:
         load.wait()
@@ -231,18 +231,27 @@
     def part(p):
         return pl.ds(pl.multiple_of(p * msg, msg), msg)
 
-    spans = [pl.ds(low * msg, (high - low) * msg) for low, high in chunks]
+    def spans_of(pairs):
+        return [pl.ds(low * msg, (high - low) * msg) for low, high in pairs]
+
+    spans, near_spans = spans_of(chunks), spans_of(near_chunks)
     a1.wait()
     mid_a[...] = dot(turn, buf_a[...].reshape(rows, feats), 1, 0).astype(BF).reshape(n, msg, feats)
-    a2 = [Arrival(mid_a.at[pl.ds(max(low, 1), high - max(low, 1))]) for low, high in chunks]
-    for (low, high), arrival in zip(chunks, a2):
+    a2 = [
+        Arrival(mid_a.at[pl.ds(max(low, 1), high - max(low, 1))]) if high > 1 else None
+        for low, high in near_chunks
+    ]
+    for (low, high), arrival in zip(near_chunks, a2):
         send_each(max(low, 1), high, arrival, lambda p: (
             mid_a.at[p], rx.at[c, x, part(p)], at_y(away(p))))
     rx[c, x, 0:msg] = mid_a[0]
     b1.wait()
     mid_b[...] = dot(turn, buf_b[...].reshape(rows, feats), 1, 0).astype(BF).reshape(n, msg, feats)
-    b2 = [Arrival(mid_b.at[pl.ds(max(low, 1), high - max(low, 1))]) for low, high in chunks]
-    for (low, high), arrival in zip(chunks, b2):
+    b2 = [
+        Arrival(mid_b.at[pl.ds(max(low, 1), high - max(low, 1))]) if high > 1 else None
+        for low, high in near_chunks
+    ]
+    for (low, high), arrival in zip(near_chunks, b2):
         send_each(max(low, 1), high, arrival, lambda p: (
             mid_b.at[p], rd.at[c, x, part(p)], at_z(away(p))))
     rd[c, x, 0:msg] = mid_b[0]
@@ -289,16 +298,18 @@
     left, right = lax.rem(x + NX - 1, NX), lax.rem(x + 1, NX)
 
     def to_x(buf, at, h, k):
-        ref = buf.at[c, at, spans[h]]
+        ref = buf.at[c, at, near_spans[h]]
         arrival = Arrival(ref)
         send(ref, ref, arrival, at_x(k % NX))
         return arrival
 
     x_right, x_left, d_right, d_left = [], [], [], []
-    for h in range(len(chunks)):
-        a2[h].wait()
+    for h in range(len(near_chunks)):
+        if a2[h]:
+            a2[h].wait()
         x_right.append(to_x(rx, x, h, 1))
-        b2[h].wait()
+        if b2[h]:
+            b2[h].wait()
         d_left.append(to_x(rd, x, h, -1))
         x_left.append(to_x(rx, x, h, -1))
         d_right.append(to_x(rd, x, h, 1))
@@ -306,12 +317,13 @@
             rings_first()
 
     x_on, d_on = [], []
-    for h in range(len(chunks)):
+    for h in range(len(near_chunks)):
         x_right[h].wait()
         x_on.append(to_x(rx, left, h, 1))
         d_left[h].wait()
         d_on.append(to_x(rd, right, h, -1))
-    rings()
+        if h == 2:
+            rings()
 
     for arrival in w_sib:
         arrival.wait()

time: 59.6 us -> 58.9 us (0.988)
  Pallas kernels: 58.7 us -> 58 us
    pallas_call x1, Pallas kernels: 56.4 us -> 55.8 us  [body(): pl.pallas_call(functools.partial(kernel, n), out_shape=results, in_specs=...]
where the time goes in v4:
time: 58.9 us; the launch traced here: 58.7 us
  Pallas kernels  58 us (98%)
  between operations  0.64 us (1%)
    pallas_call x1, Pallas kernels, body(): pl.pallas_call(functools.partial(kernel, n), out_shape=results, in_specs=...  55.8 us
    pallas_call x1, Pallas kernels, body(): pl.pallas_call(hand_out, out_shape=results, in_specs=[hbm] * len(results)...  2.29 us

profile of v4, /device:TPU:1, one launch (start us, length us, event | category | flops | bytes accessed | tf_op | source)
XLA Modules:
  0.0 58.7 jit_solution(8840167415420433708)
XLA Ops:
  0.6 55.8 %shard_map.137 = (bf16[16,512]{1,0:T(8,128)(2,1)}, f32[6,16]{1,0:T(8,128)}, bf16[1,2048,128]{2,1,0:T(8,128)(2,1)}, bf16[1,2048,128]{2,1,0:T(8,128)(2,1)}, bf16[1,128,2048]{2,1,0:T(8,128)(2,1)}) custom-call(bf16[16,512]{1,0:T(8,128)(2,1)} %tok_hbm.1, bf16[16,512]{1,0:T(8,128)(2,1)} %dy_hbm.1, bf16[6,16]{1,0:T(8,128)(2,1)} %bitcast.6, s32[6,16]{1,0:T(8,128)} %bitcast.5, ...), custom_call_target="tpu_custom_call" | custom-call | tf_op jit(solution)/shard_map/pallas_call | solution.py:610
  56.4 2.3 %shard_map.138 = (bf16[16,512]{1,0:T(8,128)(2,1)}, f32[6,16]{1,0:T(8,128)}, bf16[1,2048,128]{2,1,0:T(8,128)(2,1)}, bf16[1,2048,128]{2,1,0:T(8,128)(2,1)}, bf16[1,128,2048]{2,1,0:T(8,128)(2,1)}) custom-call(bf16[16,512]{1,0:T(8,128)(2,1)} %get-tuple-element.15.refs_0_, f32[6,16]{1,0:T(8,128)} %get-tuple-element.16.refs_1_, ...), custom_call_target="tpu_custom_call" | custom-call | tf_op jit(solution)/shard_map/pallas_call | solution.py:620
